TPU v7x, 128 devices: a whole 4x4x4 slice. The times are simulated.
128 devices in a mesh: img: 32 (over z, y, core), tp: 4 (over x).
Axes of the slice: x: 4, y: 4, z: 4, core: 2. Of those that a mesh axis runs over, the one named last changes fastest.
Arguments:
- tokens: bfloat16 [128, 256, 1024], P('img', 'tp'), may hold values from -6 to 6
- image_pairs: int32 [128, 2], replicated, may hold values from 0 to 127, as said below
- image_row: int32 [128], replicated, may hold values from 0 to 127, as said below
- embed_weight: bfloat16 [1024, 768], replicated, may hold values from -0.1875 to 0.1875
- norm_gain: float32 [2, 4, 768], replicated, may hold values from 0.5 to 1.5
- norm_bias: float32 [2, 4, 768], replicated, may hold values from -2 to 2
- self_qkv: bfloat16 [2, 3, 768, 768], P(None, None, None, 'tp'), may hold values from -0.21875 to 0.21875
- self_out: bfloat16 [2, 768, 768], P(None, 'tp'), may hold values from -0.21875 to 0.21875
- cross_qkv: bfloat16 [2, 3, 768, 768], P(None, None, None, 'tp'), may hold values from -0.21875 to 0.21875
- cross_out: bfloat16 [2, 768, 768], P(None, 'tp'), may hold values from -0.21875 to 0.21875
- mlp_up: bfloat16 [2, 768, 3072], P(None, None, 'tp'), may hold values from -0.21875 to 0.21875
- mlp_down: bfloat16 [2, 3072, 768], P(None, 'tp'), may hold values from -0.109375 to 0.109375
Outputs:
- features: bfloat16 [128, 256, 768], P('img', 'tp')
Inputs may be any that keep to these rules, and one draw needn't show every extreme that they name: `image_pairs`: the two images of a pair differ. For each worker w, of the 8 images of pairs w * 4 to (w + 1) * 4 - 1, at most 1 have rows in one owner's block (rows o * 4 to (o + 1) * 4 - 1), and for every worker some owner's block holds exactly 1 of them; an image may appear more than once. `image_row`: A permutation of the rows.
All inputs are finite; a program needn't handle non-finite values.
Results may differ from a plain program's by a relative error of at most 0.014.
Values may be sent and summed in bfloat16 or wider, within the bound.
A program may use at most 128 MiB of HBM per device.

v0:
```python
import jax
import jax.numpy as jnp
from jax import lax
from jax.sharding import PartitionSpec as P

HEAD = 64


eps = 1e-06


def layer_norm(value, gain, shift):
    mean = jnp.mean(value, axis=-1, keepdims=True)
    centred = value - mean
    spread = jnp.mean(centred * centred, axis=-1, keepdims=True)
    return centred * lax.rsqrt(spread + eps) * gain + shift


def project(rows, weight):
    return jnp.einsum("bld,dx->blx", rows, weight, preferred_element_type=jnp.float32)


def attend(query, keys, values):
    count, length, width = query.shape
    heads = width // HEAD
    q_heads = query.reshape(count, length, heads, HEAD)
    k_heads = keys.reshape(count, keys.shape[1], heads, HEAD)
    v_heads = values.reshape(count, values.shape[1], heads, HEAD)
    scores = jnp.einsum(
        "bqhd,bkhd->bhqk", q_heads, k_heads, preferred_element_type=jnp.float32
    ) * HEAD ** (-0.5)
    weights = jax.nn.softmax(scores, axis=-1).astype(jnp.bfloat16)
    mixed = jnp.einsum("bhqk,bkhd->bqhd", weights, v_heads, preferred_element_type=jnp.float32)
    return mixed.reshape(count, length, width).astype(jnp.bfloat16)


def per_device(
    tokens,
    image_pairs,
    image_row,
    embed_weight,
    norm_gain,
    norm_bias,
    self_qkv,
    self_out,
    cross_qkv,
    cross_out,
    mlp_up,
    mlp_down,
):
    workers = lax.axis_size("img")
    me = lax.axis_index("img")
    part = lax.axis_index("tp")
    img_dev = tokens.shape[0]
    quarter = tokens.shape[1]
    views = 2 * image_pairs.shape[0] // workers
    slots = (views + workers - 1) // workers
    rows_all = jnp.take(image_row, image_pairs.reshape(-1), axis=0).reshape(workers, views)
    owner_of = rows_all // img_dev
    local_of = rows_all % img_dev
    order = jnp.arange(views, dtype=jnp.int32)
    earlier = order[None, :] < order[:, None]
    same_owner = owner_of[:, :, None] == owner_of[:, None, :]
    rank_of = jnp.sum(same_owner & earlier[None], axis=2)
    capacity = jnp.arange(slots, dtype=jnp.int32)
    pick = (owner_of[:, None, :] == me) & (rank_of[:, None, :] == capacity[None, :, None])
    filled = jnp.any(pick, axis=2).reshape(-1)
    source_local = jnp.sum(jnp.where(pick, local_of[:, None, :], 0), axis=2).reshape(-1)
    mine_owner = owner_of[me]
    mine_rank = rank_of[me]
    arrival = mine_owner * slots + mine_rank

    def outgoing(source, usable, index):
        picked = jnp.take(source, index, axis=0)
        keep = usable.reshape((-1,) + (1,) * (source.ndim - 1))
        return jnp.where(keep, picked, jnp.zeros_like(picked))

    arrived = lax.all_to_all(
        outgoing(tokens, filled, source_local), "img", split_axis=0, concat_axis=0, tiled=True
    )
    chosen = jnp.take(arrived, arrival, axis=0)
    start = jnp.einsum(
        "bte,ed->btd", chosen, embed_weight, preferred_element_type=jnp.float32
    ).astype(jnp.bfloat16)

    def reduce_value(parts):
        return (
            lax.psum(parts[0].astype(jnp.bfloat16), "tp").astype(jnp.float32),
            lax.psum(parts[1].astype(jnp.bfloat16), "tp").astype(jnp.float32),
        )

    inputs = lax.all_gather(start, "tp", axis=1, tiled=True)
    paired = inputs.reshape(views // 2, 2, inputs.shape[1], inputs.shape[2])
    own_input = (paired[:, 0], paired[:, 1])
    state = [own_input[0].astype(jnp.float32), own_input[1].astype(jnp.float32)]

    def normed(value, side, which):
        return layer_norm(value, norm_gain[side, which], norm_bias[side, which]).astype(
            jnp.bfloat16
        )

    held = (normed(state[0], 0, 0), normed(state[1], 1, 0))
    partials = []
    for side in range(2):
        query = project(held[side], self_qkv[side, 0]).astype(jnp.bfloat16)
        keys = project(held[side], self_qkv[side, 1]).astype(jnp.bfloat16)
        values = project(held[side], self_qkv[side, 2]).astype(jnp.bfloat16)
        partials.append(project(attend(query, keys, values), self_out[side]))
    sums = reduce_value((partials[0], partials[1]))
    state = [state[0] + sums[0], state[1] + sums[1]]
    held = (
        normed(state[0], 0, 1),
        normed(state[1], 1, 1),
        normed(own_input[1].astype(jnp.float32), 0, 2),
        normed(own_input[0].astype(jnp.float32), 1, 2),
    )
    partials = []
    for side in range(2):
        query = project(held[side], cross_qkv[side, 0]).astype(jnp.bfloat16)
        keys = project(held[2 + side], cross_qkv[side, 1]).astype(jnp.bfloat16)
        values = project(held[2 + side], cross_qkv[side, 2]).astype(jnp.bfloat16)
        partials.append(project(attend(query, keys, values), cross_out[side]))
    sums = reduce_value((partials[0], partials[1]))
    state = [state[0] + sums[0], state[1] + sums[1]]
    held = (normed(state[0], 0, 3), normed(state[1], 1, 3))
    partials = []
    for side in range(2):
        hidden = jax.nn.gelu(project(held[side], mlp_up[side]), approximate=False).astype(
            jnp.bfloat16
        )
        partials.append(project(hidden, mlp_down[side]))
    sums = reduce_value((partials[0], partials[1]))
    state = [state[0] + sums[0], state[1] + sums[1]]
    finished = jnp.stack(state, axis=1)
    finished = finished.reshape(views, finished.shape[2], finished.shape[3])
    finished = lax.dynamic_slice_in_dim(finished, part * quarter, quarter, 1)
    owners_range = jnp.arange(workers, dtype=jnp.int32)
    back_pick = (mine_owner[None, None, :] == owners_range[:, None, None]) & (
        mine_rank[None, None, :] == capacity[None, :, None]
    )
    back_valid = jnp.any(back_pick, axis=2).reshape(-1)
    back_slot = jnp.sum(jnp.where(back_pick, order[None, None, :], 0), axis=2).reshape(-1)
    returned = lax.all_to_all(
        outgoing(finished, back_valid, back_slot).astype(jnp.bfloat16),
        "img",
        split_axis=0,
        concat_axis=0,
        tiled=True,
    ).astype(jnp.float32)
    table = (
        (source_local[None, :] == jnp.arange(img_dev, dtype=jnp.int32)[:, None]) & filled[None, :]
    ).astype(jnp.float32)
    total = jnp.einsum("im,mtd->itd", table, returned, precision=lax.Precision.HIGHEST)
    return total.astype(jnp.bfloat16)


def solution(mesh):
    in_specs = (
        P("img", "tp", None),
        P(),
        P(),
        P(),
        P(),
        P(),
        P(None, None, None, "tp"),
        P(None, "tp", None),
        P(None, None, None, "tp"),
        P(None, "tp", None),
        P(None, None, "tp"),
        P(None, "tp", None),
    )
    out_specs = P("img", "tp", None)
    return jax.shard_map(
        per_device, mesh=mesh, in_specs=in_specs, out_specs=out_specs, check_vma=False
    )
```

profile of v0, /device:TPU:1, one launch (start us, length us, event | category | flops | bytes accessed | tf_op | source)
XLA Modules:
  0.0 543.9 jit_solution(2609538710667918836)
XLA Ops:
  7.7 1.9 gather_fusion
  10.4 2.8 gather_fusion.1
  13.2 4.7 select_select_fusion
  17.9 9.7 %all-to-all-start = ((bf16[32,64,1024]{2,1,0:T(8,128)(2,1)}), bf16[32,64,1024]{2,1,0:T(8,128)(2,1)}, u32[]{:S(2)}, u32[]{:S(2)}) async-start(bf16[32,64,1024]{2,1,0:T(8,128)(2,1)} %select_select_fusion), calls=%async_computation | async-start | bytes 8388608 | tf_op jit(solution)/shard_map/all_to_all | solution.py:78
  27.8 50.0 %all-to-all-done = bf16[32,64,1024]{2,1,0:T(8,128)(2,1)} async-done(((bf16[32,64,1024]{2,1,0:T(8,128)(2,1)}), bf16[32,64,1024]{2,1,0:T(8,128)(2,1)}, u32[]{:S(2)}, u32[]{:S(2)}) %all-to-all-start) | async-done | bytes 4194336 | tf_op jit(solution)/shard_map/all_to_all | solution.py:78
  77.8 2.8 gather_fusion.2
  80.6 1.9 fusion.88
  82.8 39.1 %all-gather.2.cloned.1.call-done = bf16[8,256,768]{2,1,0:T(8,128)(2,1)} async-done(((bf16[8,64,768]{2,1,0:T(8,128)(2,1)}), bf16[8,256,768]{2,1,0:T(8,128)(2,1)}) %all-gather.2.cloned.1.call-update) | async-done | bytes 3145744 | tf_op jit(solution)/shard_map/all_gather | solution.py:92
  121.8 2.5 convert_reduce_fusion
  125.3 2.7 convolution_convert_fusion.13
  127.9 2.6 convolution_convert_fusion.14
  130.6 2.6 convolution_convert_fusion.15
  133.2 4.0 fusion.256
  137.2 2.5 fusion.94
  139.7 1.8 convolution_convert_fusion.5
  141.7 50.5 %all-reduce.7.cloned.1.call-done = bf16[4,256,768]{2,1,0:T(8,128)(2,1)} async-done(((bf16[4,256,768]{2,1,0:T(8,128)(2,1)}), bf16[4,256,768]{2,1,0:T(8,128)(2,1)}) %all-reduce.7.cloned.1.call-update) | async-done | bytes 1572880 | tf_op jit(solution)/shard_map/psum | solution.py:88
  192.2 2.0 fusion.59
  197.3 1.7 convolution_convert_fusion.9
  200.8 2.7 convolution_convert_fusion.11
  203.5 2.7 convolution_convert_fusion.12
  206.1 4.0 fusion.258
  210.1 2.6 fusion.92
  212.7 1.9 convolution_convert_fusion.2
  214.5 2.9 fusion.99
  217.4 4.0 fusion.257
  221.4 2.5 fusion.93
  223.9 1.8 convolution_convert_fusion.4
  225.9 2.7 convolution_convert_fusion.6
  228.6 2.6 convolution_convert_fusion.7
  231.2 70.7 %all-reduce.13.cloned.1.call-done = (bf16[4,256,768]{2,1,0:T(8,128)(2,1)}, bf16[4,256,768]{2,1,0:T(8,128)(2,1)}) async-done(((bf16[4,256,768]{2,1,0:T(8,128)(2,1)}, bf16[4,256,768]{2,1,0:T(8,128)(2,1)}), (bf16[4,256,768]{2,1,0:T(8,128)(2,1)}, bf16[4,256,768]{2,1,0:T(8,128)(2,1)})) %all-reduce.13.cloned.1.call-update) | async-done | bytes 3145744 | tf_op jit(solution)/shard_map/psum | solution.py:88
  302.0 3.6 fusion.253
  306.3 2.9 fusion.98
  309.2 4.0 fusion.259
  313.2 2.5 fusion.91
  315.7 1.8 convolution_convert_fusion.1
  317.9 49.8 %all-reduce.9.cloned.1.call-done = bf16[4,256,768]{2,1,0:T(8,128)(2,1)} async-done(((bf16[4,256,768]{2,1,0:T(8,128)(2,1)}), bf16[4,256,768]{2,1,0:T(8,128)(2,1)}) %all-reduce.9.cloned.1.call-update) | async-done | bytes 1572880 | tf_op jit(solution)/shard_map/psum | solution.py:89
  367.7 2.7 fusion.254
  371.0 3.1 multiply_reduce_fusion.2
  374.2 2.7 fusion.116
  377.0 9.3 %convolution_convert_fusion.3 = bf16[4,256,768]{2,1,0:T(8,128)(2,1)} fusion(f32[4,256,768]{2,1,0:T(8,128)S(1)} %get-tuple-element.55, bf16[2,768,768]{2,1,0:T(8,128)(2,1)S(1)} %copy-done.18, u8[256,768]{1,0:T(8,128)(4,1)S(1)} %get-tuple-element.6, u8[256,768]{1,0:T(8,128)(4,1)S(1)} %get-tuple-element.5), kind=kOutput, calls=%fused_computation.117 | convolution fusion | flops 1263796224 | bytes 6291456 | tf_op jit(solution)/shard_map/bld,dx->blx/dot_general | solution.py:20
  386.3 2.7 fusion.117
  389.0 9.5 %convolution_convert_fusion = bf16[4,256,768]{2,1,0:T(8,128)(2,1)} fusion(f32[4,256,768]{2,1,0:T(8,128)S(1)} %get-tuple-element.54, bf16[2,768,768]{2,1,0:T(8,128)(2,1)S(1)} %copy-done.18, u8[256,768]{1,0:T(8,128)(4,1)S(1)} %get-tuple-element.14, u8[256,768]{1,0:T(8,128)(4,1)S(1)} %get-tuple-element.13), kind=kOutput, calls=%fused_computation.114 | convolution fusion | flops 1263796224 | bytes 6291456 | tf_op jit(solution)/shard_map/bld,dx->blx/dot_general | solution.py:20
  398.8 76.1 %all-reduce.11.cloned.1.call-done = (bf16[4,256,768]{2,1,0:T(8,128)(2,1)}, bf16[4,256,768]{2,1,0:T(8,128)(2,1)}) async-done(((bf16[4,256,768]{2,1,0:T(8,128)(2,1)}, bf16[4,256,768]{2,1,0:T(8,128)(2,1)}), (bf16[4,256,768]{2,1,0:T(8,128)(2,1)}, bf16[4,256,768]{2,1,0:T(8,128)(2,1)})) %all-reduce.11.cloned.1.call-update) | async-done | bytes 3145744 | tf_op jit(solution)/shard_map/psum | solution.py:89
  474.8 5.3 add_bitcast_fusion.1
  480.8 2.4 gather_fusion.3
  483.2 3.5 select_convert_fusion
  486.7 47.3 %all_to_all.10 = bf16[32,64,768]{2,1,0:T(8,128)(2,1)S(1)} all-to-all(bf16[32,64,768]{2,1,0:T(8,128)(2,1)S(1)} %select_convert_fusion), channel_id=1, replica_groups=mesh['img'=32,'tp'=4] {'img'}, dimensions={0} | all-to-all | bytes 6291456 | tf_op jit(solution)/shard_map/all_to_all | solution.py:143
  534.0 2.4 fusion.95
  (100 shorter events, 12.1 us)
Async XLA Ops:
  6.5 74.1 %copy-start = (bf16[1024,768]{1,0:T(8,128)(2,1)S(1)}, bf16[1024,768]{1,0:T(8,128)(2,1)}, u32[]{:S(2)}) copy-start(bf16[1024,768]{1,0:T(8,128)(2,1)} %param.15) | copy-start | bytes 4718596
  6.5 3.8 copy-start.8
  17.9 59.9 %all-to-all-start = ((bf16[32,64,1024]{2,1,0:T(8,128)(2,1)}), bf16[32,64,1024]{2,1,0:T(8,128)(2,1)}, u32[]{:S(2)}, u32[]{:S(2)}) async-start(bf16[32,64,1024]{2,1,0:T(8,128)(2,1)} %select_select_fusion), calls=%async_computation | async-start | bytes 8388608 | tf_op jit(solution)/shard_map/all_to_all | solution.py:78
  27.5 94.3 %all-gather.2.cloned.1.call-start = ((), (), s32[]{:S(2)}) async-start(), calls=%async_computation.2 | async-start | bytes 3932160 | tf_op jit(solution)/shard_map/all_gather | solution.py:92
  80.6 2.0 copy-start.15
  80.6 2.0 copy-start.16
  82.6 109.6 %all-reduce.7.cloned.1.call-start = ((), (), s32[]{:S(2)}) async-start(), calls=%async_computation.3 | async-start | bytes 3145728 | tf_op jit(solution)/shard_map/psum | solution.py:88
  121.8 2.8 copy-start.2
  137.2 2.5 copy-start.11
  141.5 160.5 %all-reduce.13.cloned.1.call-start = ((), (), s32[]{:S(2)}) async-start(), calls=%async_computation.6 | async-start | bytes 6291456 | tf_op jit(solution)/shard_map/psum | solution.py:88
  192.2 2.0 copy-start.3
  194.2 1.5 copy-start.19
  210.1 2.6 copy-start.12
  210.1 4.4 copy-start.4
  221.4 2.5 copy-start.13
  225.7 142.0 %all-reduce.9.cloned.1.call-start = ((), (), s32[]{:S(2)}) async-start(), calls=%async_computation.4 | async-start | bytes 3145728 | tf_op jit(solution)/shard_map/psum | solution.py:89
  302.0 3.6 copy-start.6
  313.2 2.5 copy-start.14
  317.5 157.4 %all-reduce.11.cloned.1.call-start = ((), (), s32[]{:S(2)}) async-start(), calls=%async_computation.5 | async-start | bytes 6291456 | tf_op jit(solution)/shard_map/psum | solution.py:89
  367.7 2.7 copy-start.5
  367.7 2.8 copy-start.7
  367.7 3.3 copy-start.9
  371.0 3.2 copy-start.17
  374.2 2.8 copy-start.18
  377.0 9.3 %copy-start.10 = (bf16[4,256,768]{2,1,0:T(8,128)(2,1)S(1)}, bf16[4,256,768]{2,1,0:T(8,128)(2,1)}, u32[]{:S(2)}) copy-start(bf16[4,256,768]{2,1,0:T(8,128)(2,1)} %all-reduce.9.cloned.1.call-done) | copy-start | bytes 4718596
  486.7 50.5 %copy-start.1 = (bf16[1024,768]{1,0:T(8,128)(2,1)S(1)}, bf16[1024,768]{1,0:T(8,128)(2,1)}, u32[]{:S(2)}) copy-start(bf16[1024,768]{1,0:T(8,128)(2,1)} %param.15) | copy-start | bytes 4718596
Sparse Core Ops, SparseCore 0:
  82.7 39.1 all-gather.1
  141.6 50.5 all-reduce.6
  225.8 76.1 all-reduce.12
  317.6 50.1 all-reduce.8
  398.7 76.0 all-reduce.10
where the time goes:
time: 551 us; the launch traced here: 544 us
  waiting for transfers between devices  336 us (61%)
  matrix products  91.1 us (17%)
  blocking collectives  47.3 us (9%)
  other arithmetic  31.1 us (6%)
  local copies, waits for them, and re-layouts  13.8 us (3%)
  between operations  13.8 us (3%)
  starting transfers between devices  10.7 us (2%)
    psum x2, waiting for transfers between devices, reduce_value(): lax.psum(parts[1].astype(jnp.bfloat16), 'tp').astype(jnp.float32)  126 us
    psum x2, waiting for transfers between devices, reduce_value(): lax.psum(parts[0].astype(jnp.bfloat16), 'tp').astype(jnp.float32)  121 us
    dot_general x20, matrix products, project(): jnp.einsum('bld,dx->blx', rows, weight, preferred_element_type=jnp.float32)  61 us
    all_to_all x1, waiting for transfers between devices, per_device(): lax.all_to_all(outgoing(tokens, filled, source_local), 'img', split_axis=...  50 us
    all_to_all x1, blocking collectives, per_device(): lax.all_to_all(outgoing(finished, back_valid, back_slot).astype(jnp.bfloa...  47.3 us
    all_gather x1, waiting for transfers between devices, per_device(): inputs = lax.all_gather(start, 'tp', axis=1, tiled=True)  39.1 us
    sub x4, matrix products, attend(): weights = jax.nn.softmax(scores, axis=-1).astype(jnp.bfloat16)  15.9 us
  transfers between devices with their start and end apart: 6, of which 6 were waited for; matrix products, arithmetic and copies ran while one was open for 1% of the time, Pallas kernels for 0%

commit v1 on v0

v1 whole, which is shorter than its diff:
```python
import jax
import jax.numpy as jnp
from jax import lax
from jax.experimental import pallas as pl
from jax.experimental.pallas import tpu as pltpu
from jax.sharding import PartitionSpec as P

D = 768
HEAD = 64
ROWS = 64
IMG = 32
TP = 4
VIEWS = 8
EPS = 1e-06
MESH = pl.DeviceIdType.MESH

WEIGHTS = ((768, 1152), (192, 768), (192, 768), (768, 768), (768, 768))


def layer_norm(value, gain, shift):
    mean = jnp.mean(value, axis=-1, keepdims=True)
    centred = value - mean
    spread = jnp.mean(centred * centred, axis=-1, keepdims=True)
    return (centred * lax.rsqrt(spread + EPS) * gain + shift).astype(jnp.bfloat16)


def dot(a, b):
    return jnp.dot(a, b, preferred_element_type=jnp.float32)


def attend(q, k, v):
    scores = lax.dot_general(q, k, (((1,), (1,)), ((), ())), preferred_element_type=jnp.float32)
    scores = scores * HEAD**-0.5
    top = jnp.max(scores, axis=-1, keepdims=True)
    weights = jnp.exp(scores - top)
    total = jnp.sum(weights, axis=-1, keepdims=True)
    return (dot(weights.astype(jnp.bfloat16), v) / total).astype(jnp.bfloat16)


def kernel(
    index_ref,
    tokens_ref,
    embed_ref,
    gain_ref,
    bias_ref,
    attn_ref,
    self_out_ref,
    cross_out_ref,
    up_ref,
    down_ref,
    out_ref,
    w_attn,
    w_so,
    w_co,
    w_up,
    w_down,
    embedded,
    send_in,
    recv_in,
    pair_send,
    pair_recv,
    state,
    normed,
    partner,
    mixed,
    unit_send,
    unit_recv,
    send_out,
    recv_out,
    own_sem,
    ring_send,
    ring_recv,
    a2a_send,
    a2a_recv,
    pair_sems,
):
    me = lax.axis_index("img")
    t = lax.axis_index("tp")
    core = lax.rem(me, 2)
    side = lax.rem(me // 8, 2)
    base = me - 8 * side
    sibling = me + 1 - 2 * core
    right = lax.rem(t + 1, TP)
    left = lax.rem(t + 3, TP)
    across = lax.rem(t + 2, TP)

    barrier = pltpu.get_barrier_semaphore()

    def greet_plane(step, carry):
        pl.semaphore_signal(
            barrier, inc=1, device_id=(lax.rem(me + step, IMG), t), device_id_type=MESH
        )
        return carry

    lax.fori_loop(1, IMG, greet_plane, 0)
    for unit in range(2):
        for step in range(1, TP):
            pl.semaphore_signal(
                barrier,
                inc=1,
                device_id=(base + 8 * unit, lax.rem(t + step, TP)),
                device_id_type=MESH,
            )
    pl.semaphore_wait(barrier, IMG - 1 + 2 * (TP - 1))

    sources = (
        attn_ref,
        self_out_ref.at[side],
        cross_out_ref.at[side],
        up_ref.at[side],
        down_ref.at[side],
    )
    held = (w_attn, w_so, w_co, w_up, w_down)

    def local(i):
        return pltpu.make_async_copy(sources[i], held[i].at[t], own_sem.at[i])

    def piece(i, kind):
        rows = WEIGHTS[i][0]
        half, part = rows // 2, rows // 4
        begin = core * half
        here = held[i]
        if kind == 0:
            src, dst, to = sources[i].at[pl.ds(begin, half)], here.at[t, pl.ds(begin, half)], (me, right)
        elif kind == 1:
            src, dst, to = sources[i].at[pl.ds(begin, half)], here.at[t, pl.ds(begin, half)], (me, left)
        elif kind == 2:
            src = dst = here.at[left, pl.ds(begin, part)]
            to = (me, right)
        elif kind == 3:
            src = dst = here.at[right, pl.ds(begin + part, part)]
            to = (me, left)
        elif kind == 4:
            src = dst = here.at[left, pl.ds(begin, half)]
            to = (sibling, t)
        elif kind == 5:
            src = dst = here.at[right, pl.ds(begin, half)]
            to = (sibling, t)
        else:
            src = dst = here.at[across, pl.ds(begin, half)]
            to = (sibling, t)
        return pltpu.make_async_remote_copy(
            src_ref=src,
            dst_ref=dst,
            send_sem=ring_send.at[i, kind],
            recv_sem=ring_recv.at[i, kind],
            device_id=to,
            device_id_type=MESH,
        )

    def begin_ring(i):
        piece(i, 0).start()
        piece(i, 1).start()
        local(i).start()

    def forward_ring(i):
        piece(i, 0).wait_recv()
        piece(i, 2).start()
        piece(i, 4).start()
        piece(i, 1).wait_recv()
        piece(i, 3).start()
        piece(i, 5).start()

    def share_ring(i):
        piece(i, 2).wait_recv()
        piece(i, 3).wait_recv()
        piece(i, 6).start()

    def finish_ring(i):
        local(i).wait()
        piece(i, 4).wait_recv()
        piece(i, 5).wait_recv()
        piece(i, 6).wait_recv()

    begin_ring(0)
    begin_ring(1)

    for image in range(4):
        embedded[image] = dot(tokens_ref[image], embed_ref[...]).astype(jnp.bfloat16)

    def slot_in(dest):
        return pltpu.make_async_remote_copy(
            src_ref=send_in.at[dest],
            dst_ref=recv_in.at[me],
            send_sem=a2a_send.at[0],
            recv_sem=a2a_recv.at[0],
            device_id=(dest, t),
            device_id_type=MESH,
        )

    def send_slot(step, carry):
        dest = lax.rem(me + step, IMG)
        send_in[dest] = embedded[index_ref[dest]]
        slot_in(dest).start()
        return carry

    lax.fori_loop(1, IMG, send_slot, 0)
    recv_in[me] = embedded[index_ref[me]]

    begin_ring(2)
    forward_ring(0)
    forward_ring(1)
    begin_ring(3)
    share_ring(0)
    share_ring(1)
    forward_ring(2)
    begin_ring(4)

    def whole(ref, sem):
        return pltpu.make_async_copy(ref.at[pl.ds(0, IMG - 1)], ref.at[pl.ds(0, IMG - 1)], sem)

    whole(recv_in, a2a_recv.at[0]).wait()

    for view in range(VIEWS):
        pair_send[view // 2, view % 2] = recv_in[index_ref[IMG + view]]

    def pair_copy(flip, step):
        pair = lax.rem(t + step, TP)
        to = base + 8 * (side + flip - 2 * side * flip)
        return pltpu.make_async_remote_copy(
            src_ref=pair_send.at[pair],
            dst_ref=pair_recv.at[side, t],
            send_sem=pair_sems.at[0, flip, step],
            recv_sem=pair_sems.at[1, flip, step],
            device_id=(to, pair),
            device_id_type=MESH,
        )

    others = [(flip, step) for step in range(TP) for flip in (1, 0) if flip or step]
    for flip, step in others:
        pair_copy(flip, step).start()
    pair_recv[side, t] = pair_send[t]
    share_ring(2)
    forward_ring(3)
    for flip, step in others:
        pair_copy(flip, step).wait_recv()

    for unit in range(2):
        for quarter in range(TP):
            rows = pl.ds(unit * 256 + quarter * ROWS, ROWS)
            state[rows, :] = pair_recv[unit, quarter, side].astype(jnp.float32)
            partner[rows, :] = pair_recv[unit, quarter, 1 - side]

    def norm(value, which):
        return layer_norm(value, gain_ref[side, pl.ds(which, 1)], bias_ref[side, pl.ds(which, 1)])

    for unit in range(2):
        rows = pl.ds(unit * 256, 256)
        normed[rows, :] = norm(state[rows, :], 0)
        partner[rows, :] = norm(partner[rows, :].astype(jnp.float32), 2)

    finish_ring(0)
    finish_ring(1)

    def heads(q, k, v):
        for unit in range(2):
            rows = slice(unit * 256, unit * 256 + 256)
            parts = []
            for head in range(3):
                columns = slice(head * HEAD, head * HEAD + HEAD)
                parts.append(attend(q[rows, columns], k[rows, columns], v[rows, columns]))
            mixed[rows, :] = jnp.concatenate(parts, axis=1)

    def self_group(group, carry):
        qkv = dot(normed[...], w_attn[group, :, 0:640]).astype(jnp.bfloat16)
        heads(qkv[:, 0:192], qkv[:, 192:384], qkv[:, 384:576])
        state[...] += dot(mixed[...], w_so[group])
        return carry

    lax.fori_loop(0, TP, self_group, 0)

    share_ring(3)
    forward_ring(4)
    for unit in range(2):
        rows = pl.ds(unit * 256, 256)
        normed[rows, :] = norm(state[rows, :], 1)
    finish_ring(2)

    def cross_group(group, carry):
        q = dot(normed[...], w_attn[group, :, 512:768]).astype(jnp.bfloat16)
        kv = dot(partner[...], w_attn[group, :, 768:1152]).astype(jnp.bfloat16)
        heads(q[:, 64:256], kv[:, 0:192], kv[:, 192:384])
        state[...] += dot(mixed[...], w_co[group])
        return carry

    lax.fori_loop(0, TP, cross_group, 0)

    share_ring(4)
    for unit in range(2):
        rows = pl.ds(unit * 256, 256)
        normed[rows, :] = norm(state[rows, :], 3)
    finish_ring(3)
    finish_ring(4)

    def mlp_group(group, carry):
        hidden = dot(normed[...], w_up[group])
        hidden = hidden * (lax.erf(hidden * 0.5**0.5) + 1.0) * 0.5
        state[...] += dot(hidden.astype(jnp.bfloat16), w_down[group])
        return carry

    lax.fori_loop(0, TP, mlp_group, 0)

    for unit in range(2):
        for quarter in range(TP):
            rows = pl.ds(unit * 256 + quarter * ROWS, ROWS)
            unit_send[unit, quarter] = state[rows, :].astype(jnp.bfloat16)

    def unit_copy(flip, step):
        quarter = lax.rem(t + step, TP)
        unit = side + flip - 2 * side * flip
        return pltpu.make_async_remote_copy(
            src_ref=unit_send.at[unit, quarter],
            dst_ref=unit_recv.at[t, side],
            send_sem=pair_sems.at[2, flip, step],
            recv_sem=pair_sems.at[3, flip, step],
            device_id=(base + 8 * unit, quarter),
            device_id_type=MESH,
        )

    for flip, step in others:
        unit_copy(flip, step).start()
    unit_recv[t, side] = unit_send[side, t]
    for flip, step in others:
        unit_copy(flip, step).wait_recv()

    def slot_out(dest):
        return pltpu.make_async_remote_copy(
            src_ref=send_out.at[dest],
            dst_ref=recv_out.at[me],
            send_sem=a2a_send.at[1],
            recv_sem=a2a_recv.at[1],
            device_id=(dest, t),
            device_id_type=MESH,
        )

    def send_back(step, carry):
        dest = lax.rem(me + step, IMG)
        view = index_ref[IMG + VIEWS + dest]
        send_out[dest] = unit_recv[view // 2, lax.rem(view, 2)]
        slot_out(dest).start()
        return carry

    lax.fori_loop(1, IMG, send_back, 0)
    view_here = index_ref[IMG + VIEWS + me]
    recv_out[me] = unit_recv[view_here // 2, lax.rem(view_here, 2)]

    for i in range(len(WEIGHTS)):
        for kind in range(7):
            piece(i, kind).wait_send()
    for flip, step in others:
        pair_copy(flip, step).wait_send()
        unit_copy(flip, step).wait_send()
    whole(send_in, a2a_send.at[0]).wait()
    whole(recv_out, a2a_recv.at[1]).wait()

    def add_rows(chunk, carry):
        rows = pl.ds(pl.multiple_of(chunk * 16, 16), 16)
        sums = [jnp.zeros((16, D), jnp.float32) for _ in range(4)]
        for worker in range(IMG):
            value = recv_out[worker, rows, :].astype(jnp.float32)
            image_here = index_ref[2 * IMG + VIEWS + worker]
            for image in range(4):
                sums[image] += jnp.where(image_here == image, value, 0.0)
        for image in range(4):
            out_ref[image, rows, :] = sums[image].astype(jnp.bfloat16)
        return carry

    lax.fori_loop(0, ROWS // 16, add_rows, 0)
    whole(send_out, a2a_send.at[1]).wait()


def per_device(
    tokens,
    image_pairs,
    image_row,
    embed_weight,
    norm_gain,
    norm_bias,
    self_qkv,
    self_out,
    cross_qkv,
    cross_out,
    mlp_up,
    mlp_down,
):
    me = lax.axis_index("img")
    side = lax.rem(me // 8, 2)
    img_dev = tokens.shape[0]
    rows_all = jnp.take(image_row, image_pairs.reshape(-1), axis=0).reshape(IMG, VIEWS)
    owner = rows_all // img_dev
    place = rows_all % img_dev
    from_me = owner == me
    wanted = jnp.sum(jnp.where(from_me, place, 0), axis=1)
    filled = jnp.any(from_me, axis=1)
    mine = owner[me]
    views = jnp.arange(VIEWS, dtype=jnp.int32)
    workers = jnp.arange(IMG, dtype=jnp.int32)
    back = jnp.sum(jnp.where(mine[None, :] == workers[:, None], views[None, :], 0), axis=1)
    index = jnp.concatenate([wanted, mine, back, jnp.where(filled, wanted, -1)]).astype(jnp.int32)

    qkv = jnp.concatenate(
        [
            lax.dynamic_index_in_dim(self_qkv, side, 0, keepdims=False),
            lax.dynamic_index_in_dim(cross_qkv, side, 0, keepdims=False),
        ],
        axis=0,
    )
    attn = jnp.transpose(qkv, (1, 0, 2)).reshape(D, 6 * 192)

    bf16 = jnp.bfloat16
    vmem = pl.BlockSpec(memory_space=pltpu.VMEM)
    hbm = pl.BlockSpec(memory_space=pl.ANY)
    return pl.pallas_call(
        kernel,
        out_shape=jax.ShapeDtypeStruct((img_dev, ROWS, D), bf16),
        in_specs=[pl.BlockSpec(memory_space=pltpu.SMEM)] + [vmem] * 4 + [hbm] * 5,
        out_specs=vmem,
        scratch_shapes=[pltpu.VMEM((TP,) + shape, bf16) for shape in WEIGHTS]
        + [
            pltpu.VMEM((4, ROWS, D), bf16),
            pltpu.VMEM((IMG, ROWS, D), bf16),
            pltpu.VMEM((IMG, ROWS, D), bf16),
            pltpu.VMEM((4, 2, ROWS, D), bf16),
            pltpu.VMEM((2, TP, 2, ROWS, D), bf16),
            pltpu.VMEM((512, D), jnp.float32),
            pltpu.VMEM((512, D), bf16),
            pltpu.VMEM((512, D), bf16),
            pltpu.VMEM((512, 192), bf16),
            pltpu.VMEM((2, TP, ROWS, D), bf16),
            pltpu.VMEM((4, 2, ROWS, D), bf16),
            pltpu.VMEM((IMG, ROWS, D), bf16),
            pltpu.VMEM((IMG, ROWS, D), bf16),
            pltpu.SemaphoreType.DMA((len(WEIGHTS),)),
            pltpu.SemaphoreType.DMA((len(WEIGHTS), 7)),
            pltpu.SemaphoreType.DMA((len(WEIGHTS), 7)),
            pltpu.SemaphoreType.DMA((2,)),
            pltpu.SemaphoreType.DMA((2,)),
            pltpu.SemaphoreType.DMA((4, 2, TP)),
        ],
        compiler_params=pltpu.CompilerParams(
            collective_id=0, has_side_effects=True, vmem_limit_bytes=60 * 1024 * 1024
        ),
    )(index, tokens, embed_weight, norm_gain, norm_bias, attn, self_out, cross_out, mlp_up, mlp_down)


def solution(mesh):
    in_specs = (
        P("img", "tp", None),
        P(),
        P(),
        P(),
        P(),
        P(),
        P(None, None, None, "tp"),
        P(None, "tp", None),
        P(None, None, None, "tp"),
        P(None, "tp", None),
        P(None, None, "tp"),
        P(None, "tp", None),
    )
    out_specs = P("img", "tp", None)
    return jax.shard_map(
        per_device, mesh=mesh, in_specs=in_specs, out_specs=out_specs, check_vma=False
    )
```

time: 551 us -> 203 us (0.37); the launches traced: 544 us -> 203 us
  waiting for transfers between devices: 336 us -> 0 us
  Pallas kernels: 0 us -> 193 us
  matrix products: 91.1 us -> 0 us
  blocking collectives: 47.3 us -> 0 us
  other arithmetic: 31.1 us -> 1.13 us
  between operations: 13.8 us -> 0.08 us
  starting transfers between devices: 10.7 us -> 0 us
    psum x4 -> x0, waiting for transfers between devices: 247 us -> none  [the longest x2 126 us: reduce_value(): lax.psum(parts[1].astype(jnp.bfloat16), 'tp').astype(jnp.float32)]
    pallas_call x0 -> x1, Pallas kernels: none -> 193 us  [per_device(): pl.pallas_call(kernel, out_shape=jax.ShapeDtypeStruct((img_dev, ROWS, D),...]
    dot_general x26 -> x0, matrix products: 75.2 us -> none  [the longest x20 61 us: project(): jnp.einsum('bld,dx->blx', rows, weight, preferred_element_type=jnp.float32)]
    all_to_all x1 -> x0, waiting for transfers between devices: 50 us -> none  [per_device(): lax.all_to_all(outgoing(tokens, filled, source_local), 'img', split_axis=...]
    all_to_all x1 -> x0, blocking collectives: 47.3 us -> none  [per_device(): lax.all_to_all(outgoing(finished, back_valid, back_slot).astype(jnp.bfloa...]
    all_gather x1 -> x0, waiting for transfers between devices: 39.1 us -> none  [per_device(): inputs = lax.all_gather(start, 'tp', axis=1, tiled=True)]
    reduce_sum x11 -> x2, other arithmetic: 16.8 us -> 0.25 us  [the longest x1 0.14 us: per_device(): wanted = jnp.sum(jnp.where(from_me, place, 0), axis=1)]
    sub x4 -> x0, matrix products: 15.9 us -> none  [attend(): weights = jax.nn.softmax(scores, axis=-1).astype(jnp.bfloat16)]
  transfers between devices with their start and end apart: 6 -> 0, of which waited for: 6 -> 0; matrix products, arithmetic and copies ran while one was open for 1% -> 0% of each run, Pallas kernels for 0% -> 0%
where the time goes in v1:
time: 203 us
  Pallas kernels  193 us (95%)
  local copies, waits for them, and re-layouts  8.53 us (4%)
    pallas_call x1, Pallas kernels, per_device(): pl.pallas_call(kernel, out_shape=jax.ShapeDtypeStruct((img_dev, ROWS, D),...  193 us

profile of v1, /device:TPU:1, one launch (start us, length us, event | category | flops | bytes accessed | tf_op | source)
XLA Modules:
  0.0 202.8 jit_solution(7422690107157789653)
XLA Ops:
  0.0 0.0 copy-start
  0.0 0.8 copy.13
  0.8 0.1 reshape.46
  0.9 0.1 reshape.45
  1.0 0.0 copy-done
  1.1 1.9 gather_fusion
  2.9 0.1 gather.7
  3.0 0.1 fusion.1
  3.1 0.1 reduce_or.9
  3.3 0.1 select_reduce_fusion
  3.4 0.6 pad_add_fusion.index_ref
  4.0 1.5 dynamic-slice_bitcast_fusion
  5.6 0.2 pad_maximum_fusion
  5.7 2.2 %copy.15.attn_ref = bf16[768,1152]{1,0:T(8,128)(2,1)} copy(bf16[768,1152]{0,1:T(8,128)(2,1)S(1)} %bitcast.10) | data formatting | bytes 3538944 | tf_op jit(solution)/shard_map/reshape | solution.py:408
  8.0 193.1 %shard_map.118 = bf16[4,64,768]{2,1,0:T(8,128)(2,1)} custom-call(s32[104]{0:T(128)} %pad_add_fusion.index_ref, bf16[4,64,1024]{2,1,0:T(8,128)(2,1)} %tokens_ref.1, bf16[1024,768]{1,0:T(8,128)(2,1)} %embed_ref.1, f32[2,4,768]{2,1,0:T(4,128)} %gain_ref.1, f32[2,4,768]{2,1,0:T(4,128)} %bias_ref.1, bf16[768,1152]{1,0:T(8,128)(2,1)} %copy.15.attn_ref, ...), custom_call_target="tpu_custom_call" | custom-call | tf_op jit(solution)/shard_map/pallas_call | solution.py:413
  201.1 1.8 copy.17
  (4 shorter events, 0.0 us)
Async XLA Ops:
  0.0 1.0 copy-start

commit v2 on v1

--- a/solution.py
+++ b/solution.py
@@ -15,6 +15,13 @@
 MESH = pl.DeviceIdType.MESH
 
 WEIGHTS = ((768, 1152), (192, 768), (192, 768), (768, 768), (768, 768))
+
+
+ALONG = (
+    (1, 1), (3, 3), (1, 3), (3, 1), (2, 2), (1, 0), (0, 1), (3, 0),
+    (0, 3), (2, 1), (1, 2), (2, 3), (3, 2), (2, 0), (0, 2), (0, 0),
+)
+STEPS = [(z, y, c) for c in range(2) for z, y in ALONG if z or y or c]
 
 
 def layer_norm(value, gain, shift):
@@ -77,12 +84,20 @@
     me = lax.axis_index("img")
     t = lax.axis_index("tp")
     core = lax.rem(me, 2)
-    side = lax.rem(me // 8, 2)
-    base = me - 8 * side
+    y = lax.rem(me // 2, 4)
+    z = me // 8
+    side = lax.rem(z, 2)
     sibling = me + 1 - 2 * core
     right = lax.rem(t + 1, TP)
     left = lax.rem(t + 3, TP)
     across = lax.rem(t + 2, TP)
+
+    def at(step):
+        other = core + step[2] - 2 * core * step[2]
+        return (lax.rem(z + step[0], 4) * 4 + lax.rem(y + step[1], 4)) * 2 + other
+
+    giver = lax.rem(me + 24 - 16 * core, IMG)
+    taker = lax.rem(me + 8 + 16 * core, IMG)
 
     barrier = pltpu.get_barrier_semaphore()
 
@@ -93,15 +108,12 @@
         return carry
 
     lax.fori_loop(1, IMG, greet_plane, 0)
-    for unit in range(2):
+    for worker in (me, giver, taker):
         for step in range(1, TP):
             pl.semaphore_signal(
-                barrier,
-                inc=1,
-                device_id=(base + 8 * unit, lax.rem(t + step, TP)),
-                device_id_type=MESH,
+                barrier, inc=1, device_id=(worker, lax.rem(t + step, TP)), device_id_type=MESH
             )
-    pl.semaphore_wait(barrier, IMG - 1 + 2 * (TP - 1))
+    pl.semaphore_wait(barrier, IMG - 1 + 3 * (TP - 1))
 
     sources = (
         attn_ref,
@@ -115,62 +127,85 @@
     def local(i):
         return pltpu.make_async_copy(sources[i], held[i].at[t], own_sem.at[i])
 
-    def piece(i, kind):
+    def split(i):
+        return 2 if i < 3 else 4
+
+    def piece(i, kind, quarter=None):
         rows = WEIGHTS[i][0]
-        half, part = rows // 2, rows // 4
-        begin = core * half
+        block = rows // split(i)
+        half = block // 2
+        mine = core if i < 3 else 2 * lax.rem(y, 2) + core
+        theirs = core if i < 3 else 2 - 2 * lax.rem(y, 2) + core
         here = held[i]
-        if kind == 0:
-            src, dst, to = sources[i].at[pl.ds(begin, half)], here.at[t, pl.ds(begin, half)], (me, right)
-        elif kind == 1:
-            src, dst, to = sources[i].at[pl.ds(begin, half)], here.at[t, pl.ds(begin, half)], (me, left)
-        elif kind == 2:
-            src = dst = here.at[left, pl.ds(begin, part)]
-            to = (me, right)
-        elif kind == 3:
-            src = dst = here.at[right, pl.ds(begin + part, part)]
-            to = (me, left)
-        elif kind == 4:
-            src = dst = here.at[left, pl.ds(begin, half)]
-            to = (sibling, t)
-        elif kind == 5:
-            src = dst = here.at[right, pl.ds(begin, half)]
-            to = (sibling, t)
+        which = {"left": left, "right": right, "across": across}.get(quarter)
+        n = ("left", "right", "across").index(quarter) if quarter else 0
+        if kind == "send":
+            begin, count, to = mine * block, block, (me, right if quarter == "left" else left)
+            src, dst, sem = sources[i], here.at[t], n
+        elif kind == "pass":
+            begin = mine * block + (0 if quarter == "left" else half)
+            count, to = half, (me, right if quarter == "left" else left)
+            src, dst, sem = here.at[which], here.at[which], 2 + n
+        elif kind == "core":
+            begin, count, to = mine * block, block, (sibling, t)
+            src, dst, sem = here.at[which], here.at[which], 4 + n
+        elif kind == "up":
+            begin, count, to = mine * block, half, (at((0, 1, 0)), t)
+            src, dst, sem = here.at[which], here.at[which], 7 + n
+        elif kind == "down":
+            begin, count, to = mine * block + half, half, (at((0, 3, 0)), t)
+            src, dst, sem = here.at[which], here.at[which], 10 + n
         else:
-            src = dst = here.at[across, pl.ds(begin, half)]
-            to = (sibling, t)
+            begin, count, to = theirs * block, block, (sibling, t)
+            src, dst, sem = here.at[which], here.at[which], 13 + n
         return pltpu.make_async_remote_copy(
-            src_ref=src,
-            dst_ref=dst,
-            send_sem=ring_send.at[i, kind],
-            recv_sem=ring_recv.at[i, kind],
+            src_ref=src.at[pl.ds(begin, count)],
+            dst_ref=dst.at[pl.ds(begin, count)],
+            send_sem=ring_send.at[i, sem],
+            recv_sem=ring_recv.at[i, sem],
             device_id=to,
             device_id_type=MESH,
         )
 
+    def spread(i, quarter):
+        for kind in ("core",) if i < 3 else ("up", "down", "core"):
+            piece(i, kind, quarter).start()
+
     def begin_ring(i):
-        piece(i, 0).start()
-        piece(i, 1).start()
+        piece(i, "send", "left").start()
+        piece(i, "send", "right").start()
         local(i).start()
 
     def forward_ring(i):
-        piece(i, 0).wait_recv()
-        piece(i, 2).start()
-        piece(i, 4).start()
-        piece(i, 1).wait_recv()
-        piece(i, 3).start()
-        piece(i, 5).start()
+        for quarter in ("left", "right"):
+            piece(i, "send", quarter).wait_recv()
+            piece(i, "pass", quarter).start()
+            spread(i, quarter)
 
     def share_ring(i):
-        piece(i, 2).wait_recv()
-        piece(i, 3).wait_recv()
-        piece(i, 6).start()
+        piece(i, "pass", "left").wait_recv()
+        piece(i, "pass", "right").wait_recv()
+        spread(i, "across")
+
+    def swap_ring(i, quarter):
+        piece(i, "up", quarter).wait_recv()
+        piece(i, "down", quarter).wait_recv()
+        piece(i, "swap", quarter).start()
 
     def finish_ring(i):
         local(i).wait()
-        piece(i, 4).wait_recv()
-        piece(i, 5).wait_recv()
-        piece(i, 6).wait_recv()
+        for quarter in ("left", "right", "across"):
+            piece(i, "core", quarter).wait_recv()
+            if i >= 3:
+                piece(i, "swap", quarter).wait_recv()
+
+    def drain_ring(i):
+        for quarter in ("left", "right", "across"):
+            if quarter != "across":
+                piece(i, "send", quarter).wait_send()
+                piece(i, "pass", quarter).wait_send()
+            for kind in ("core",) if i < 3 else ("up", "down", "core", "swap"):
+                piece(i, kind, quarter).wait_send()
 
     begin_ring(0)
     begin_ring(1)
@@ -178,62 +213,75 @@
     for image in range(4):
         embedded[image] = dot(tokens_ref[image], embed_ref[...]).astype(jnp.bfloat16)
 
-    def slot_in(dest):
+    def slot(way, send, recv, step):
+        dest = at(step)
         return pltpu.make_async_remote_copy(
-            src_ref=send_in.at[dest],
-            dst_ref=recv_in.at[me],
-            send_sem=a2a_send.at[0],
-            recv_sem=a2a_recv.at[0],
+            src_ref=send.at[dest],
+            dst_ref=recv.at[me],
+            send_sem=a2a_send.at[way],
+            recv_sem=a2a_recv.at[way],
             device_id=(dest, t),
             device_id_type=MESH,
         )
 
-    def send_slot(step, carry):
-        dest = lax.rem(me + step, IMG)
-        send_in[dest] = embedded[index_ref[dest]]
-        slot_in(dest).start()
-        return carry
-
-    lax.fori_loop(1, IMG, send_slot, 0)
-    recv_in[me] = embedded[index_ref[me]]
-
-    begin_ring(2)
-    forward_ring(0)
-    forward_ring(1)
-    begin_ring(3)
-    share_ring(0)
-    share_ring(1)
-    forward_ring(2)
-    begin_ring(4)
+    def send_slots(way, send, recv, fill):
+        for step in STEPS:
+            send[at(step)] = fill(at(step))
+            slot(way, send, recv, step).start()
+        recv[me] = fill(me)
 
     def whole(ref, sem):
         return pltpu.make_async_copy(ref.at[pl.ds(0, IMG - 1)], ref.at[pl.ds(0, IMG - 1)], sem)
 
+    send_slots(0, send_in, recv_in, lambda dest: embedded[index_ref[dest]])
+
+    forward_ring(0)
+    begin_ring(2)
+    forward_ring(1)
+    share_ring(0)
+    forward_ring(2)
+    share_ring(1)
+
     whole(recv_in, a2a_recv.at[0]).wait()
 
     for view in range(VIEWS):
         pair_send[view // 2, view % 2] = recv_in[index_ref[IMG + view]]
 
-    def pair_copy(flip, step):
+    def pair_copy(step):
         pair = lax.rem(t + step, TP)
-        to = base + 8 * (side + flip - 2 * side * flip)
         return pltpu.make_async_remote_copy(
             src_ref=pair_send.at[pair],
-            dst_ref=pair_recv.at[side, t],
-            send_sem=pair_sems.at[0, flip, step],
-            recv_sem=pair_sems.at[1, flip, step],
-            device_id=(to, pair),
+            dst_ref=pair_recv.at[0, t],
+            send_sem=pair_sems.at[0, 0, step],
+            recv_sem=pair_sems.at[0, 1, step],
+            device_id=(me, pair),
             device_id_type=MESH,
         )
 
-    others = [(flip, step) for step in range(TP) for flip in (1, 0) if flip or step]
-    for flip, step in others:
-        pair_copy(flip, step).start()
-    pair_recv[side, t] = pair_send[t]
+    def pair_pass(step):
+        quarter = lax.rem(t + TP - step, TP)
+        return pltpu.make_async_remote_copy(
+            src_ref=pair_recv.at[0, quarter],
+            dst_ref=pair_recv.at[1, quarter],
+            send_sem=pair_sems.at[1, 0, step],
+            recv_sem=pair_sems.at[1, 1, step],
+            device_id=(taker, t),
+            device_id_type=MESH,
+        )
+
+    for step in (2, 1, 3):
+        pair_copy(step).start()
+    pair_recv[0, t] = pair_send[t]
+    pair_pass(0).start()
+    begin_ring(3)
+    for step in (1, 3, 2):
+        pair_copy(step).wait_recv()
+        pair_pass(step).start()
     share_ring(2)
+    begin_ring(4)
     forward_ring(3)
-    for flip, step in others:
-        pair_copy(flip, step).wait_recv()
+    for step in range(TP):
+        pair_pass(step).wait_recv()
 
     for unit in range(2):
         for quarter in range(TP):
@@ -262,6 +310,16 @@
             mixed[rows, :] = jnp.concatenate(parts, axis=1)
 
     def self_group(group, carry):
+        @pl.when(group == 1)
+        def _():
+            share_ring(3)
+
+        @pl.when(group == 2)
+        def _():
+            forward_ring(4)
+            swap_ring(3, "left")
+            swap_ring(3, "right")
+
         qkv = dot(normed[...], w_attn[group, :, 0:640]).astype(jnp.bfloat16)
         heads(qkv[:, 0:192], qkv[:, 192:384], qkv[:, 384:576])
         state[...] += dot(mixed[...], w_so[group])
@@ -269,14 +327,22 @@
 
     lax.fori_loop(0, TP, self_group, 0)
 
-    share_ring(3)
-    forward_ring(4)
     for unit in range(2):
         rows = pl.ds(unit * 256, 256)
         normed[rows, :] = norm(state[rows, :], 1)
     finish_ring(2)
 
     def cross_group(group, carry):
+        @pl.when(group == 0)
+        def _():
+            share_ring(4)
+            swap_ring(3, "across")
+
+        @pl.when(group == 2)
+        def _():
+            swap_ring(4, "left")
+            swap_ring(4, "right")
+
         q = dot(normed[...], w_attn[group, :, 512:768]).astype(jnp.bfloat16)
         kv = dot(partner[...], w_attn[group, :, 768:1152]).astype(jnp.bfloat16)
         heads(q[:, 64:256], kv[:, 0:192], kv[:, 192:384])
@@ -285,7 +351,7 @@
 
     lax.fori_loop(0, TP, cross_group, 0)
 
-    share_ring(4)
+    swap_ring(4, "across")
     for unit in range(2):
         rows = pl.ds(unit * 256, 256)
         normed[rows, :] = norm(state[rows, :], 3)
@@ -305,51 +371,38 @@
             rows = pl.ds(unit * 256 + quarter * ROWS, ROWS)
             unit_send[unit, quarter] = state[rows, :].astype(jnp.bfloat16)
 
-    def unit_copy(flip, step):
+    def unit_copy(unit, step):
         quarter = lax.rem(t + step, TP)
-        unit = side + flip - 2 * side * flip
         return pltpu.make_async_remote_copy(
             src_ref=unit_send.at[unit, quarter],
             dst_ref=unit_recv.at[t, side],
-            send_sem=pair_sems.at[2, flip, step],
-            recv_sem=pair_sems.at[3, flip, step],
-            device_id=(base + 8 * unit, quarter),
+            send_sem=pair_sems.at[2 + unit, 0, step],
+            recv_sem=pair_sems.at[2 + unit, 1, step],
+            device_id=((me, giver)[unit], quarter),
             device_id_type=MESH,
         )
 
-    for flip, step in others:
-        unit_copy(flip, step).start()
-    unit_recv[t, side] = unit_send[side, t]
-    for flip, step in others:
-        unit_copy(flip, step).wait_recv()
-
-    def slot_out(dest):
-        return pltpu.make_async_remote_copy(
-            src_ref=send_out.at[dest],
-            dst_ref=recv_out.at[me],
-            send_sem=a2a_send.at[1],
-            recv_sem=a2a_recv.at[1],
-            device_id=(dest, t),
-            device_id_type=MESH,
-        )
-
-    def send_back(step, carry):
-        dest = lax.rem(me + step, IMG)
+    others = [(unit, step) for step in (2, 1, 3, 0) for unit in (1, 0) if unit or step]
+    for unit, step in others:
+        unit_copy(unit, step).start()
+    unit_recv[t, side] = unit_send[0, t]
+    for unit, step in others:
+        unit_copy(unit, step).wait_recv()
+
+    def view_for(dest):
         view = index_ref[IMG + VIEWS + dest]
-        send_out[dest] = unit_recv[view // 2, lax.rem(view, 2)]
-        slot_out(dest).start()
-        return carry
-
-    lax.fori_loop(1, IMG, send_back, 0)
-    view_here = index_ref[IMG + VIEWS + me]
-    recv_out[me] = unit_recv[view_here // 2, lax.rem(view_here, 2)]
+        return unit_recv[view // 2, lax.rem(view, 2)]
+
+    send_slots(1, send_out, recv_out, view_for)
 
     for i in range(len(WEIGHTS)):
-        for kind in range(7):
-            piece(i, kind).wait_send()
-    for flip, step in others:
-        pair_copy(flip, step).wait_send()
-        unit_copy(flip, step).wait_send()
+        drain_ring(i)
+    for step in range(TP):
+        if step:
+            pair_copy(step).wait_send()
+        pair_pass(step).wait_send()
+    for unit, step in others:
+        unit_copy(unit, step).wait_send()
     whole(send_in, a2a_send.at[0]).wait()
     whole(recv_out, a2a_recv.at[1]).wait()
 
@@ -431,8 +484,8 @@
             pltpu.VMEM((IMG, ROWS, D), bf16),
             pltpu.VMEM((IMG, ROWS, D), bf16),
             pltpu.SemaphoreType.DMA((len(WEIGHTS),)),
-            pltpu.SemaphoreType.DMA((len(WEIGHTS), 7)),
-            pltpu.SemaphoreType.DMA((len(WEIGHTS), 7)),
+            pltpu.SemaphoreType.DMA((len(WEIGHTS), 16)),
+            pltpu.SemaphoreType.DMA((len(WEIGHTS), 16)),
             pltpu.SemaphoreType.DMA((2,)),
             pltpu.SemaphoreType.DMA((2,)),
             pltpu.SemaphoreType.DMA((4, 2, TP)),

time: 203 us -> 170 us (0.84)
  Pallas kernels: 193 us -> 160 us
    pallas_call x1, Pallas kernels: 193 us -> 160 us  [per_device(): pl.pallas_call(kernel, out_shape=jax.ShapeDtypeStruct((img_dev, ROWS, D),...]
where the time goes in v2:
time: 170 us
  Pallas kernels  160 us (94%)
  local copies, waits for them, and re-layouts  8.53 us (5%)
    pallas_call x1, Pallas kernels, per_device(): pl.pallas_call(kernel, out_shape=jax.ShapeDtypeStruct((img_dev, ROWS, D),...  160 us

profile of v2, /device:TPU:1, one launch (start us, length us, event | category | flops | bytes accessed | tf_op | source)
XLA Modules:
  0.0 169.6 jit_solution(8097330167446177317)
XLA Ops:
  0.0 0.0 copy-start
  0.0 0.8 copy.13
  0.8 0.1 reshape.46
  0.9 0.1 reshape.45
  1.0 0.0 copy-done
  1.1 1.9 %gather_fusion = s32[256]{0:T(256)S(1)} fusion(s32[128]{0:T(128)S(1)} %copy-done, s32[1024]{0:T(1024)S(1)} %pad_clamp_fusion), kind=kCustom, calls=%fused_computation | custom fusion | bytes 3072 | tf_op jit(solution)/shard_map/jit(_take)/gather | solution.py:442
  2.9 0.1 gather.7
  3.0 0.1 fusion.1
  3.1 0.1 reduce_or.9
  3.3 0.1 select_reduce_fusion
  3.4 0.6 pad_add_fusion.index_ref
  4.0 1.5 dynamic-slice_bitcast_fusion
  5.6 0.2 pad_maximum_fusion
  5.7 2.2 %copy.15.attn_ref = bf16[768,1152]{1,0:T(8,128)(2,1)} copy(bf16[768,1152]{0,1:T(8,128)(2,1)S(1)} %bitcast.10) | data formatting | bytes 3538944 | tf_op jit(solution)/shard_map/reshape | solution.py:461
  8.0 159.9 %shard_map.118 = bf16[4,64,768]{2,1,0:T(8,128)(2,1)} custom-call(s32[104]{0:T(128)} %pad_add_fusion.index_ref, bf16[4,64,1024]{2,1,0:T(8,128)(2,1)} %tokens_ref.1, bf16[1024,768]{1,0:T(8,128)(2,1)} %embed_ref.1, f32[2,4,768]{2,1,0:T(4,128)} %gain_ref.1, f32[2,4,768]{2,1,0:T(4,128)} %bias_ref.1, bf16[768,1152]{1,0:T(8,128)(2,1)} %copy.15.attn_ref, ...), custom_call_target="tpu_custom_call" | custom-call | tf_op jit(solution)/shard_map/pallas_call | solution.py:466
  167.8 1.8 %copy.17 = bf16[4,64,768]{2,1,0:T(8,128)(2,1)} copy(bf16[4,64,768]{2,1,0:T(8,128)(2,1)} %shard_map.118) | data formatting | bytes 786432
  (4 shorter events, 0.0 us)
Async XLA Ops:
  0.0 1.0 copy-start

commit v3 on v2

v3 whole, which is shorter than its diff:
```python
import functools

import jax
import jax.numpy as jnp
from jax import lax
from jax.experimental import pallas as pl
from jax.experimental.pallas import tpu as pltpu
from jax.sharding import PartitionSpec as P

D = 768
HEAD = 64
ROWS = 64
PART = 32
IMG = 32
TP = 4
VIEWS = 8
EPS = 1e-06
MESH = pl.DeviceIdType.MESH

SHARE = (192, 192, 192, 192, 768, 768)
UP, DOWN = 4, 5


ALONG = (
    (1, 1), (3, 3), (1, 3), (3, 1), (2, 2), (1, 0), (0, 1), (3, 0),
    (0, 3), (2, 1), (1, 2), (2, 3), (3, 2), (2, 0), (0, 2), (0, 0),
)
STEPS = [(z, y, c) for c in range(2) for z, y in ALONG if z or y or c]


QUARTERS = ("own", "right", "left", "across")


def layer_norm(value, gain, shift):
    mean = jnp.mean(value, axis=-1, keepdims=True)
    centred = value - mean
    spread = jnp.mean(centred * centred, axis=-1, keepdims=True)
    return (centred * lax.rsqrt(spread + EPS) * gain + shift).astype(jnp.bfloat16)


def dot(a, b):
    return jnp.dot(a, b, preferred_element_type=jnp.float32)


def dot_t(a, b):
    return lax.dot_general(a, b, (((1,), (1,)), ((), ())), preferred_element_type=jnp.float32)


def attend(q, k, v):
    scores = dot_t(q, k)
    scores = scores * HEAD**-0.5
    top = jnp.max(scores, axis=-1, keepdims=True)
    weights = jnp.exp(scores - top)
    total = jnp.sum(weights, axis=-1, keepdims=True)
    return (dot(weights.astype(jnp.bfloat16), v) / total).astype(jnp.bfloat16)


def kernel(
    pairs_ref,
    row_ref,
    tokens_ref,
    embed_ref,
    gain_ref,
    bias_ref,
    self_qkv_ref,
    cross_qkv_ref,
    self_out_ref,
    cross_out_ref,
    up_ref,
    down_ref,
    out_ref,
    w_self,
    w_so,
    w_cross,
    w_co,
    w_up,
    w_down,
    embedded,
    send_in,
    recv_in_0,
    recv_in_1,
    pair_send,
    pair_recv,
    state,
    normed,
    partner,
    mixed,
    unit_send,
    unit_recv_0,
    unit_recv_1,
    send_out,
    recv_out_0,
    recv_out_1,
    wanted_ref,
    mine_ref,
    back_ref,
    own_sem,
    ring_send,
    ring_recv,
    a2a_send,
    a2a_recv,
    pair_sems,
):
    me = lax.axis_index("img")
    t = lax.axis_index("tp")
    core = lax.rem(me, 2)
    y = lax.rem(me // 2, 4)
    z = me // 8
    side = lax.rem(z, 2)
    sibling = me + 1 - 2 * core
    right = lax.rem(t + 1, TP)
    left = lax.rem(t + 3, TP)
    across = lax.rem(t + 2, TP)

    def at(step):
        other = core + step[2] - 2 * core * step[2]
        return (lax.rem(z + step[0], 4) * 4 + lax.rem(y + step[1], 4)) * 2 + other

    giver = lax.rem(me + 24 - 16 * core, IMG)
    taker = lax.rem(me + 8 + 16 * core, IMG)

    sources = (
        self_qkv_ref.at[side],
        self_out_ref.at[side],
        cross_qkv_ref.at[side],
        cross_out_ref.at[side],
        up_ref.at[side],
        down_ref.at[side],
    )
    held = (w_self, w_so, w_cross, w_co, w_up, w_down)

    def local(i):
        return pltpu.make_async_copy(sources[i], held[i].at[t], own_sem.at[i])

    for i in range(len(SHARE)):
        local(i).start()

    barrier = pltpu.get_barrier_semaphore()

    def greet_plane(step, carry):
        pl.semaphore_signal(
            barrier, inc=1, device_id=(lax.rem(me + step, IMG), t), device_id_type=MESH
        )
        return carry

    lax.fori_loop(1, IMG, greet_plane, 0)
    for worker in (me, giver, taker):
        for step in range(1, TP):
            pl.semaphore_signal(
                barrier, inc=1, device_id=(worker, lax.rem(t + step, TP)), device_id_type=MESH
            )

    def row_of(worker, view):
        return row_ref[pairs_ref[view % 2, worker * 4 + view // 2]]

    def find_wanted(worker, carry):
        found = 0
        for view in range(VIEWS):
            row = row_of(worker, view)
            found = jnp.maximum(found, jnp.where(row // 4 == me, lax.rem(row, 4) + 1, 0))
        wanted_ref[worker] = found
        return carry

    lax.fori_loop(0, IMG, find_wanted, 0)
    for view in range(VIEWS):
        mine_ref[view] = row_of(me, view) // 4

    def find_back(owner, carry):
        found = 0
        for view in range(VIEWS):
            found = jnp.maximum(found, jnp.where(mine_ref[view] == owner, view, 0))
        back_ref[owner] = found
        return carry

    lax.fori_loop(0, IMG, find_back, 0)

    for image in range(4):
        embedded[image] = dot(tokens_ref[image], embed_ref[...]).astype(jnp.bfloat16)

    pl.semaphore_wait(barrier, IMG - 1 + 3 * (TP - 1))

    def split(i):
        return 2 if i < UP else 4

    def piece(i, kind, quarter=None):
        block = SHARE[i] // split(i)
        half = block // 2
        mine = core if i < UP else 2 * lax.rem(y, 2) + core
        theirs = core if i < UP else 2 - 2 * lax.rem(y, 2) + core
        here = held[i]
        which = {"left": left, "right": right, "across": across}.get(quarter)
        n = ("left", "right", "across").index(quarter) if quarter else 0
        if kind == "send":
            begin, count, to = mine * block, block, (me, right if quarter == "left" else left)
            src, dst, sem = sources[i], here.at[t], n
        elif kind == "pass":
            begin = mine * block + (0 if quarter == "left" else half)
            count, to = half, (me, right if quarter == "left" else left)
            src, dst, sem = here.at[which], here.at[which], 2 + n
        elif kind == "core":
            begin, count, to = mine * block, block, (sibling, t)
            src, dst, sem = here.at[which], here.at[which], 4 + n
        elif kind == "up":
            begin, count, to = mine * block, half, (at((0, 1, 0)), t)
            src, dst, sem = here.at[which], here.at[which], 7 + n
        elif kind == "down":
            begin, count, to = mine * block + half, half, (at((0, 3, 0)), t)
            src, dst, sem = here.at[which], here.at[which], 10 + n
        else:
            begin, count, to = theirs * block, block, (sibling, t)
            src, dst, sem = here.at[which], here.at[which], 13 + n
        rows = pl.ds(begin, count)
        if i in (0, 2):
            rows = (slice(None), rows)
        return pltpu.make_async_remote_copy(
            src_ref=src.at[rows],
            dst_ref=dst.at[rows],
            send_sem=ring_send.at[i, sem],
            recv_sem=ring_recv.at[i, sem],
            device_id=to,
            device_id_type=MESH,
        )

    def spread(i, quarter):
        for kind in ("core",) if i < UP else ("up", "down", "core"):
            piece(i, kind, quarter).start()

    def begin_ring(i):
        piece(i, "send", "left").start()
        piece(i, "send", "right").start()

    def forward_ring(i):
        for quarter in ("left", "right"):
            piece(i, "send", quarter).wait_recv()
            piece(i, "pass", quarter).start()
            spread(i, quarter)

    def share_ring(i):
        piece(i, "pass", "left").wait_recv()
        piece(i, "pass", "right").wait_recv()
        spread(i, "across")

    def swap_ring(i, quarter):
        piece(i, "up", quarter).wait_recv()
        piece(i, "down", quarter).wait_recv()
        piece(i, "swap", quarter).start()

    def finish_ring(i, quarter):
        if quarter == "own":
            local(i).wait()
            return
        piece(i, "core", quarter).wait_recv()
        if i >= UP:
            piece(i, "swap", quarter).wait_recv()

    def drain_ring(i):
        for quarter in ("left", "right", "across"):
            if quarter != "across":
                piece(i, "send", quarter).wait_send()
                piece(i, "pass", quarter).wait_send()
            for kind in ("core",) if i < UP else ("up", "down", "core", "swap"):
                piece(i, kind, quarter).wait_send()

    begin_ring(0)
    begin_ring(1)

    recv_in = (recv_in_0, recv_in_1)
    unit_recv = (unit_recv_0, unit_recv_1)
    recv_out = (recv_out_0, recv_out_1)

    def slot(way, send, recv, step, part):
        dest = at(step)
        rows = pl.ds(part * PART, PART)
        return pltpu.make_async_remote_copy(
            src_ref=send.at[dest, rows],
            dst_ref=recv[part].at[me],
            send_sem=a2a_send.at[way, part],
            recv_sem=a2a_recv.at[way, part],
            device_id=(dest, t),
            device_id_type=MESH,
        )

    def send_slots(way, send, recv, part, fill):
        rows = pl.ds(part * PART, PART)
        for step in STEPS:
            send[at(step), rows, :] = fill(at(step), rows)
            slot(way, send, recv, step, part).start()
        recv[part][me] = fill(me, rows)

    def whole(ref, sems, way, part):
        some = ref.at[pl.ds(0, IMG - 1)]
        if ref.shape[1] == ROWS:
            some = ref.at[pl.ds(0, IMG - 1), pl.ds(part * PART, PART)]
        pltpu.make_async_copy(some, some, sems.at[way, part]).wait()

    def image_for(dest, rows):
        return embedded[jnp.maximum(wanted_ref[dest] - 1, 0), rows, :]

    send_slots(0, send_in, recv_in, 0, image_for)
    begin_ring(2)
    begin_ring(3)
    send_slots(0, send_in, recv_in, 1, image_for)
    forward_ring(0)
    forward_ring(1)

    def pair_copy(step, part):
        pair = lax.rem(t + step, TP)
        return pltpu.make_async_remote_copy(
            src_ref=pair_send.at[pair, part],
            dst_ref=pair_recv.at[0, t, part],
            send_sem=pair_sems.at[0, part, 0, step],
            recv_sem=pair_sems.at[0, part, 1, step],
            device_id=(me, pair),
            device_id_type=MESH,
        )

    def pair_pass(step, part):
        quarter = lax.rem(t + TP - step, TP)
        return pltpu.make_async_remote_copy(
            src_ref=pair_recv.at[0, quarter, part],
            dst_ref=pair_recv.at[1, quarter, part],
            send_sem=pair_sems.at[1, part, 0, step],
            recv_sem=pair_sems.at[1, part, 1, step],
            device_id=(taker, t),
            device_id_type=MESH,
        )

    def begin_pairs(part):
        whole(recv_in[part], a2a_recv, 0, part)
        for view in range(VIEWS):
            pair_send[view // 2, part, view % 2] = recv_in[part][mine_ref[view]]
        for step in (2, 1, 3):
            pair_copy(step, part).start()
        pair_recv[0, t, part] = pair_send[t, part]
        pair_pass(0, part).start()

    def pass_pairs(part):
        for step in (1, 3, 2):
            pair_copy(step, part).wait_recv()
            pair_pass(step, part).start()

    def take_unit(unit, part):
        for quarter in range(TP):
            rows = pl.ds(unit * 256 + part * 128 + quarter * PART, PART)
            state[rows, :] = pair_recv[unit, quarter, part, side].astype(jnp.float32)
            partner[rows, :] = pair_recv[unit, quarter, part, 1 - side]
        rows = pl.ds(unit * 256 + part * 128, 128)
        normed[rows, :] = norm(state[rows, :], 0)
        partner[rows, :] = norm(partner[rows, :].astype(jnp.float32), 2)

    def norm(value, which):
        return layer_norm(value, gain_ref[side, pl.ds(which, 1)], bias_ref[side, pl.ds(which, 1)])

    begin_pairs(0)
    share_ring(0)
    share_ring(1)
    forward_ring(2)
    pass_pairs(0)
    take_unit(0, 0)
    forward_ring(3)
    begin_ring(UP)
    begin_pairs(1)
    begin_ring(DOWN)
    for step in range(TP):
        pair_pass(step, 0).wait_recv()
    take_unit(1, 0)
    pass_pairs(1)
    share_ring(2)
    share_ring(3)
    take_unit(0, 1)
    forward_ring(UP)
    for step in range(TP):
        pair_pass(step, 1).wait_recv()
    take_unit(1, 1)

    for i in range(2):
        for quarter in QUARTERS:
            finish_ring(i, quarter)

    def heads(q, k, v):
        for unit in range(2):
            rows = slice(unit * 256, unit * 256 + 256)
            parts = []
            for head in range(3):
                columns = slice(head * HEAD, head * HEAD + HEAD)
                parts.append(attend(q[rows, columns], k[rows, columns], v[rows, columns]))
            mixed[rows, :] = jnp.concatenate(parts, axis=1)

    def self_group(group, carry):
        @pl.when(group == 1)
        def _():
            share_ring(UP)
            forward_ring(DOWN)

        @pl.when(group == 2)
        def _():
            swap_ring(UP, "left")
            swap_ring(UP, "right")

        @pl.when(group == 3)
        def _():
            share_ring(DOWN)
            swap_ring(UP, "across")

        qkv = dot_t(normed[...], w_self[group].reshape(576, D)).astype(jnp.bfloat16)
        heads(qkv[:, 0:192], qkv[:, 192:384], qkv[:, 384:576])
        state[...] += dot(mixed[...], w_so[group])
        return carry

    lax.fori_loop(0, TP, self_group, 0)

    for unit in range(2):
        rows = pl.ds(unit * 256, 256)
        normed[rows, :] = norm(state[rows, :], 1)
    for i in range(2, UP):
        for quarter in QUARTERS:
            finish_ring(i, quarter)

    def cross_group(group, carry):
        @pl.when(group == 0)
        def _():
            swap_ring(DOWN, "left")
            swap_ring(DOWN, "right")

        @pl.when(group == 2)
        def _():
            swap_ring(DOWN, "across")

        q = dot_t(normed[...], w_cross[group, 0]).astype(jnp.bfloat16)
        kv = dot_t(partner[...], w_cross[group, 1:3].reshape(384, D)).astype(jnp.bfloat16)
        heads(q, kv[:, 0:192], kv[:, 192:384])
        state[...] += dot(mixed[...], w_co[group])
        return carry

    lax.fori_loop(0, TP, cross_group, 0)

    for unit in range(2):
        rows = pl.ds(unit * 256, 256)
        normed[rows, :] = norm(state[rows, :], 3)

    def mlp(value, group):
        hidden = dot(value, w_up[group])
        hidden = hidden * (lax.erf(hidden * 0.5**0.5) + 1.0) * 0.5
        return dot(hidden.astype(jnp.bfloat16), w_down[group])

    finish_ring(UP, "own")
    finish_ring(DOWN, "own")

    def mlp_group(i, carry):
        @pl.when(i == 1)
        def _():
            finish_ring(UP, "right")
            finish_ring(DOWN, "right")

        @pl.when(i == 2)
        def _():
            finish_ring(UP, "left")
            finish_ring(DOWN, "left")

        state[...] += mlp(normed[...], lax.rem(t + i * (i + 1) // 2, TP))
        return carry

    lax.fori_loop(0, TP - 1, mlp_group, 0)
    finish_ring(UP, "across")
    finish_ring(DOWN, "across")

    def unit_copy(unit, step, part):
        quarter = lax.rem(t + step, TP)
        rows = pl.ds(part * PART, PART)
        return pltpu.make_async_remote_copy(
            src_ref=unit_send.at[unit, quarter, rows],
            dst_ref=unit_recv[part].at[t, side],
            send_sem=pair_sems.at[2 + unit, part, 0, step],
            recv_sem=pair_sems.at[2 + unit, part, 1, step],
            device_id=((me, giver)[unit], quarter),
            device_id_type=MESH,
        )

    others = [(unit, step) for step in (2, 1, 3, 0) for unit in (1, 0) if unit or step]

    def last_group(part, carry):
        picks = [pl.ds(pl.multiple_of(unit * 256 + part * 128, 128), 128) for unit in range(2)]
        done = mlp(jnp.concatenate([normed[rows, :] for rows in picks], axis=0), across)
        for unit in range(2):
            value = state[picks[unit], :] + done[unit * 128 : unit * 128 + 128]
            for quarter in range(TP):
                unit_send[unit, quarter, pl.ds(pl.multiple_of(part * PART, PART), PART), :] = value[
                    quarter * PART : quarter * PART + PART
                ].astype(jnp.bfloat16)
        return carry

    def begin_units(part):
        for unit, step in others:
            unit_copy(unit, step, part).start()
        rows = pl.ds(part * PART, PART)
        unit_recv[part][t, side] = unit_send[0, t, rows, :]

    def begin_return(part):
        for unit, step in others:
            unit_copy(unit, step, part).wait_recv()
        def view_for(dest, rows):
            view = back_ref[dest]
            return unit_recv[part][view // 2, lax.rem(view, 2)]

        send_slots(1, send_out, recv_out, part, view_for)

    last_group(0, 0)
    begin_units(0)
    last_group(1, 0)
    begin_units(1)
    begin_return(0)
    begin_return(1)

    for i in range(len(SHARE)):
        drain_ring(i)
    for part in range(2):
        for step in range(TP):
            if step:
                pair_copy(step, part).wait_send()
            pair_pass(step, part).wait_send()
        for unit, step in others:
            unit_copy(unit, step, part).wait_send()
        whole(send_in, a2a_send, 0, part)

    def add_rows(part, chunk, carry):
        rows = pl.ds(pl.multiple_of(chunk * 16, 16), 16)
        sums = [jnp.zeros((16, D), jnp.float32) for _ in range(4)]
        for worker in range(IMG):
            value = recv_out[part][worker, rows, :].astype(jnp.float32)
            image_here = wanted_ref[worker] - 1
            for image in range(4):
                sums[image] += jnp.where(image_here == image, value, 0.0)
        for image in range(4):
            out_ref[image, pl.ds(pl.multiple_of(part * PART + chunk * 16, 16), 16), :] = sums[image].astype(jnp.bfloat16)
        return carry

    for part in range(2):
        whole(recv_out[part], a2a_recv, 1, part)
        lax.fori_loop(0, 2, functools.partial(add_rows, part), 0)
    for part in range(2):
        whole(send_out, a2a_send, 1, part)


def per_device(
    tokens,
    image_pairs,
    image_row,
    embed_weight,
    norm_gain,
    norm_bias,
    self_qkv,
    self_out,
    cross_qkv,
    cross_out,
    mlp_up,
    mlp_down,
):
    img_dev = tokens.shape[0]
    bf16 = jnp.bfloat16
    smem = pl.BlockSpec(memory_space=pltpu.SMEM)
    vmem = pl.BlockSpec(memory_space=pltpu.VMEM)
    hbm = pl.BlockSpec(memory_space=pl.ANY)
    return pl.pallas_call(
        kernel,
        out_shape=jax.ShapeDtypeStruct((img_dev, ROWS, D), bf16),
        in_specs=[smem] * 2 + [vmem] * 4 + [hbm] * 6,
        out_specs=vmem,
        scratch_shapes=[
            pltpu.VMEM((TP, 3, SHARE[i], D) if i in (0, 2) else (TP, SHARE[i], D), bf16)
            for i in range(len(SHARE))
        ]
        + [
            pltpu.VMEM((4, ROWS, D), bf16),
            pltpu.VMEM((IMG, ROWS, D), bf16),
            pltpu.VMEM((IMG, PART, D), bf16),
            pltpu.VMEM((IMG, PART, D), bf16),
            pltpu.VMEM((4, 2, 2, PART, D), bf16),
            pltpu.VMEM((2, TP, 2, 2, PART, D), bf16),
            pltpu.VMEM((512, D), jnp.float32),
            pltpu.VMEM((512, D), bf16),
            pltpu.VMEM((512, D), bf16),
            pltpu.VMEM((512, 192), bf16),
            pltpu.VMEM((2, TP, ROWS, D), bf16),
            pltpu.VMEM((4, 2, PART, D), bf16),
            pltpu.VMEM((4, 2, PART, D), bf16),
            pltpu.VMEM((IMG, ROWS, D), bf16),
            pltpu.VMEM((IMG, PART, D), bf16),
            pltpu.VMEM((IMG, PART, D), bf16),
            pltpu.SMEM((IMG,), jnp.int32),
            pltpu.SMEM((VIEWS,), jnp.int32),
            pltpu.SMEM((IMG,), jnp.int32),
            pltpu.SemaphoreType.DMA((len(SHARE),)),
            pltpu.SemaphoreType.DMA((len(SHARE), 16)),
            pltpu.SemaphoreType.DMA((len(SHARE), 16)),
            pltpu.SemaphoreType.DMA((2, 2)),
            pltpu.SemaphoreType.DMA((2, 2)),
            pltpu.SemaphoreType.DMA((4, 2, 2, TP)),
        ],
        compiler_params=pltpu.CompilerParams(
            collective_id=0, has_side_effects=True, vmem_limit_bytes=60 * 1024 * 1024
        ),
    )(
        image_pairs.T,
        image_row,
        tokens,
        embed_weight,
        norm_gain,
        norm_bias,
        jnp.swapaxes(self_qkv, 2, 3),
        jnp.swapaxes(cross_qkv, 2, 3),
        self_out,
        cross_out,
        mlp_up,
        mlp_down,
    )


def solution(mesh):
    in_specs = (
        P("img", "tp", None),
        P(),
        P(),
        P(),
        P(),
        P(),
        P(None, None, None, "tp"),
        P(None, "tp", None),
        P(None, None, None, "tp"),
        P(None, "tp", None),
        P(None, None, "tp"),
        P(None, "tp", None),
    )
    out_specs = P("img", "tp", None)
    return jax.shard_map(
        per_device, mesh=mesh, in_specs=in_specs, out_specs=out_specs, check_vma=False
    )
```

time: 170 us -> 150 us (0.88)
  Pallas kernels: 160 us -> 147 us
  local copies, waits for them, and re-layouts: 8.53 us -> 1.77 us
    pallas_call x1, Pallas kernels: 160 us -> 147 us  [per_device(): pl.pallas_call(kernel, out_shape=jax.ShapeDtypeStruct((img_dev, ROWS, D),...]
    reshape x3 -> x0, local copies, waits for them, and re-layouts: 2.45 us -> none  [the longest x1 2.24 us: per_device(): attn = jnp.transpose(qkv, (1, 0, 2)).reshape(D, 6 * 192)]
    gather x2 -> x0, local copies, waits for them, and re-layouts: 1.95 us -> none  [per_device(): jnp.take(image_row, image_pairs.reshape(-1), axis=0).reshape(IMG, VIEWS)]
where the time goes in v3:
time: 150 us; the launch traced here: 149 us
  Pallas kernels  147 us (98%)
  local copies, waits for them, and re-layouts  1.77 us (1%)
    pallas_call x1, Pallas kernels, per_device(): pl.pallas_call(kernel, out_shape=jax.ShapeDtypeStruct((img_dev, ROWS, D),...  147 us

profile of v3, /device:TPU:1, one launch (start us, length us, event | category | flops | bytes accessed | tf_op | source)
XLA Modules:
  0.0 149.0 jit_solution(13843286778233454746)
XLA Ops:
  0.0 147.3 %shard_map.118 = bf16[4,64,768]{2,1,0:T(8,128)(2,1)} custom-call(s32[2,128]{1,0:T(2,128)} %bitcast.5, s32[128]{0:T(128)} %row_ref.1, bf16[4,64,1024]{2,1,0:T(8,128)(2,1)} %tokens_ref.1, bf16[1024,768]{1,0:T(8,128)(2,1)} %embed_ref.1, f32[2,4,768]{2,1,0:T(4,128)} %gain_ref.1, f32[2,4,768]{2,1,0:T(4,128)} %bias_ref.1, bf16[2,3,192,768]{3,2,1,0:T(8,128)(2,1)} %bitcast.3, ...), custom_call_target="tpu_custom_call" | custom-call | tf_op jit(solution)/shard_map/pallas_call | solution.py:563
  147.3 1.8 %copy.14 = bf16[4,64,768]{2,1,0:T(8,128)(2,1)} copy(bf16[4,64,768]{2,1,0:T(8,128)(2,1)} %shard_map.118) | data formatting | bytes 786432

commit v4 on v3

--- a/solution.py
+++ b/solution.py
@@ -17,7 +17,8 @@
 EPS = 1e-06
 MESH = pl.DeviceIdType.MESH
 
-SHARE = (192, 192, 192, 192, 768, 768)
+SHARE = (576, 192, 576, 192, 768, 768)
+SWAPPED = (2, 4, 5)
 UP, DOWN = 4, 5
 
 
@@ -180,13 +181,13 @@
     pl.semaphore_wait(barrier, IMG - 1 + 3 * (TP - 1))
 
     def split(i):
-        return 2 if i < UP else 4
+        return 4 if i in SWAPPED else 2
 
     def piece(i, kind, quarter=None):
         block = SHARE[i] // split(i)
-        half = block // 2
-        mine = core if i < UP else 2 * lax.rem(y, 2) + core
-        theirs = core if i < UP else 2 - 2 * lax.rem(y, 2) + core
+        half = (block + 31) // 32 * 16
+        mine = core if i not in SWAPPED else 2 * lax.rem(y, 2) + core
+        theirs = core if i not in SWAPPED else 2 - 2 * lax.rem(y, 2) + core
         here = held[i]
         which = {"left": left, "right": right, "across": across}.get(quarter)
         n = ("left", "right", "across").index(quarter) if quarter else 0
@@ -195,7 +196,8 @@
             src, dst, sem = sources[i], here.at[t], n
         elif kind == "pass":
             begin = mine * block + (0 if quarter == "left" else half)
-            count, to = half, (me, right if quarter == "left" else left)
+            count = half if quarter == "left" else block - half
+            to = (me, right if quarter == "left" else left)
             src, dst, sem = here.at[which], here.at[which], 2 + n
         elif kind == "core":
             begin, count, to = mine * block, block, (sibling, t)
@@ -204,14 +206,12 @@
             begin, count, to = mine * block, half, (at((0, 1, 0)), t)
             src, dst, sem = here.at[which], here.at[which], 7 + n
         elif kind == "down":
-            begin, count, to = mine * block + half, half, (at((0, 3, 0)), t)
+            begin, count, to = mine * block + half, block - half, (at((0, 3, 0)), t)
             src, dst, sem = here.at[which], here.at[which], 10 + n
         else:
             begin, count, to = theirs * block, block, (sibling, t)
             src, dst, sem = here.at[which], here.at[which], 13 + n
         rows = pl.ds(begin, count)
-        if i in (0, 2):
-            rows = (slice(None), rows)
         return pltpu.make_async_remote_copy(
             src_ref=src.at[rows],
             dst_ref=dst.at[rows],
@@ -221,9 +221,14 @@
             device_id_type=MESH,
         )
 
+    def offer_ring(i, quarter):
+        piece(i, "up", quarter).start()
+        piece(i, "down", quarter).start()
+
     def spread(i, quarter):
-        for kind in ("core",) if i < UP else ("up", "down", "core"):
-            piece(i, kind, quarter).start()
+        if i in (UP, DOWN):
+            offer_ring(i, quarter)
+        piece(i, "core", quarter).start()
 
     def begin_ring(i):
         piece(i, "send", "left").start()
@@ -250,7 +255,7 @@
             local(i).wait()
             return
         piece(i, "core", quarter).wait_recv()
-        if i >= UP:
+        if i in SWAPPED:
             piece(i, "swap", quarter).wait_recv()
 
     def drain_ring(i):
@@ -258,7 +263,7 @@
             if quarter != "across":
                 piece(i, "send", quarter).wait_send()
                 piece(i, "pass", quarter).wait_send()
-            for kind in ("core",) if i < UP else ("up", "down", "core", "swap"):
+            for kind in ("core",) if i not in SWAPPED else ("up", "down", "core", "swap"):
                 piece(i, kind, quarter).wait_send()
 
     begin_ring(0)
@@ -359,13 +364,15 @@
     take_unit(0, 0)
     forward_ring(3)
     begin_ring(UP)
+    share_ring(2)
     begin_pairs(1)
-    begin_ring(DOWN)
+    for quarter in QUARTERS[1:]:
+        offer_ring(2, quarter)
     for step in range(TP):
         pair_pass(step, 0).wait_recv()
     take_unit(1, 0)
     pass_pairs(1)
-    share_ring(2)
+    begin_ring(DOWN)
     share_ring(3)
     take_unit(0, 1)
     forward_ring(UP)
@@ -389,20 +396,21 @@
     def self_group(group, carry):
         @pl.when(group == 1)
         def _():
+            swap_ring(2, "right")
+            swap_ring(2, "left")
+            swap_ring(2, "across")
+
+        @pl.when(group == 2)
+        def _():
             share_ring(UP)
             forward_ring(DOWN)
 
-        @pl.when(group == 2)
+        @pl.when(group == 3)
         def _():
             swap_ring(UP, "left")
             swap_ring(UP, "right")
 
-        @pl.when(group == 3)
-        def _():
-            share_ring(DOWN)
-            swap_ring(UP, "across")
-
-        qkv = dot_t(normed[...], w_self[group].reshape(576, D)).astype(jnp.bfloat16)
+        qkv = dot_t(normed[...], w_self[group]).astype(jnp.bfloat16)
         heads(qkv[:, 0:192], qkv[:, 192:384], qkv[:, 384:576])
         state[...] += dot(mixed[...], w_so[group])
         return carry
@@ -412,22 +420,34 @@
     for unit in range(2):
         rows = pl.ds(unit * 256, 256)
         normed[rows, :] = norm(state[rows, :], 1)
-    for i in range(2, UP):
-        for quarter in QUARTERS:
-            finish_ring(i, quarter)
-
-    def cross_group(group, carry):
-        @pl.when(group == 0)
+    finish_ring(2, "own")
+    finish_ring(3, "own")
+
+    def cross_group(i, carry):
+        @pl.when(i == 0)
+        def _():
+            share_ring(DOWN)
+            swap_ring(UP, "across")
+
+        @pl.when(i == 1)
         def _():
             swap_ring(DOWN, "left")
             swap_ring(DOWN, "right")
 
-        @pl.when(group == 2)
+        @pl.when(i == 3)
         def _():
             swap_ring(DOWN, "across")
 
-        q = dot_t(normed[...], w_cross[group, 0]).astype(jnp.bfloat16)
-        kv = dot_t(partner[...], w_cross[group, 1:3].reshape(384, D)).astype(jnp.bfloat16)
+        for n in range(1, TP):
+
+            @pl.when(i == n)
+            def _():
+                finish_ring(2, QUARTERS[n])
+                finish_ring(3, QUARTERS[n])
+
+        group = lax.rem(t + i * (i + 1) // 2, TP)
+        q = dot_t(normed[...], w_cross[group, 0:192]).astype(jnp.bfloat16)
+        kv = dot_t(partner[...], w_cross[group, 192:576]).astype(jnp.bfloat16)
         heads(q, kv[:, 0:192], kv[:, 192:384])
         state[...] += dot(mixed[...], w_co[group])
         return carry
@@ -566,10 +586,7 @@
         in_specs=[smem] * 2 + [vmem] * 4 + [hbm] * 6,
         out_specs=vmem,
         scratch_shapes=[
-            pltpu.VMEM((TP, 3, SHARE[i], D) if i in (0, 2) else (TP, SHARE[i], D), bf16)
-            for i in range(len(SHARE))
-        ]
-        + [
+            *(pltpu.VMEM((TP, rows, D), bf16) for rows in SHARE),
             pltpu.VMEM((4, ROWS, D), bf16),
             pltpu.VMEM((IMG, ROWS, D), bf16),
             pltpu.VMEM((IMG, PART, D), bf16),
@@ -606,8 +623,8 @@
         embed_weight,
         norm_gain,
         norm_bias,
-        jnp.swapaxes(self_qkv, 2, 3),
-        jnp.swapaxes(cross_qkv, 2, 3),
+        jnp.swapaxes(self_qkv, 2, 3).reshape(2, 576, D),
+        jnp.swapaxes(cross_qkv, 2, 3).reshape(2, 576, D),
         self_out,
         cross_out,
         mlp_up,

time: 150 us -> 141 us (0.940)
  Pallas kernels: 147 us -> 139 us
    pallas_call x1, Pallas kernels: 147 us -> 139 us  [per_device(): pl.pallas_call(kernel, out_shape=jax.ShapeDtypeStruct((img_dev, ROWS, D),...]
where the time goes in v4:
time: 141 us
  Pallas kernels  139 us (99%)
  local copies, waits for them, and re-layouts  1.77 us (1%)
    pallas_call x1, Pallas kernels, per_device(): pl.pallas_call(kernel, out_shape=jax.ShapeDtypeStruct((img_dev, ROWS, D),...  139 us

profile of v4, /device:TPU:1, one launch (start us, length us, event | category | flops | bytes accessed | tf_op | source)
XLA Modules:
  0.0 140.7 jit_solution(12700082930399751765)
XLA Ops:
  0.0 138.9 %shard_map.118 = bf16[4,64,768]{2,1,0:T(8,128)(2,1)} custom-call(s32[2,128]{1,0:T(2,128)} %bitcast.9, s32[128]{0:T(128)} %row_ref.1, bf16[4,64,1024]{2,1,0:T(8,128)(2,1)} %tokens_ref.1, bf16[1024,768]{1,0:T(8,128)(2,1)} %embed_ref.1, f32[2,4,768]{2,1,0:T(4,128)} %gain_ref.1, f32[2,4,768]{2,1,0:T(4,128)} %bias_ref.1, bf16[2,576,768]{2,1,0:T(8,128)(2,1)} %bitcast.7, ...), custom_call_target="tpu_custom_call" | custom-call | tf_op jit(solution)/shard_map/pallas_call | solution.py:583
  138.9 1.8 %copy.14 = bf16[4,64,768]{2,1,0:T(8,128)(2,1)} copy(bf16[4,64,768]{2,1,0:T(8,128)(2,1)} %shard_map.118) | data formatting | bytes 786432

commit v5 on v4

--- a/solution.py
+++ b/solution.py
@@ -1,4 +1,5 @@
 import functools
+import math
 
 import jax
 import jax.numpy as jnp
@@ -47,13 +48,15 @@
     return lax.dot_general(a, b, (((1,), (1,)), ((), ())), preferred_element_type=jnp.float32)
 
 
-def attend(q, k, v):
-    scores = dot_t(q, k)
-    scores = scores * HEAD**-0.5
-    top = jnp.max(scores, axis=-1, keepdims=True)
-    weights = jnp.exp(scores - top)
-    total = jnp.sum(weights, axis=-1, keepdims=True)
-    return (dot(weights.astype(jnp.bfloat16), v) / total).astype(jnp.bfloat16)
+def attend(triples):
+    scores = [dot_t(q, k) for q, k, _ in triples]
+    tops = [jnp.max(score, axis=-1, keepdims=True) for score in scores]
+    weights = [jnp.exp2((score - top) * (HEAD**-0.5 * math.log2(math.e))) for score, top in zip(scores, tops)]
+    totals = [jnp.sum(weight, axis=-1, keepdims=True) for weight in weights]
+    return [
+        (dot(weight.astype(jnp.bfloat16), v) / total).astype(jnp.bfloat16)
+        for weight, total, (_, _, v) in zip(weights, totals, triples)
+    ]
 
 
 def kernel(
@@ -158,13 +161,13 @@
         found = 0
         for view in range(VIEWS):
             row = row_of(worker, view)
-            found = jnp.maximum(found, jnp.where(row // 4 == me, lax.rem(row, 4) + 1, 0))
+            found = jnp.maximum(found, jnp.where(row >> 2 == me, (row & 3) + 1, 0))
         wanted_ref[worker] = found
         return carry
 
     lax.fori_loop(0, IMG, find_wanted, 0)
     for view in range(VIEWS):
-        mine_ref[view] = row_of(me, view) // 4
+        mine_ref[view] = row_of(me, view) >> 2
 
     def find_back(owner, carry):
         found = 0
@@ -175,8 +178,8 @@
 
     lax.fori_loop(0, IMG, find_back, 0)
 
-    for image in range(4):
-        embedded[image] = dot(tokens_ref[image], embed_ref[...]).astype(jnp.bfloat16)
+    start = dot(tokens_ref[...].reshape(4 * ROWS, tokens_ref.shape[2]), embed_ref[...])
+    embedded[...] = start.astype(jnp.bfloat16).reshape(4, ROWS, D)
 
     pl.semaphore_wait(barrier, IMG - 1 + 3 * (TP - 1))
 
@@ -371,8 +374,8 @@
     for step in range(TP):
         pair_pass(step, 0).wait_recv()
     take_unit(1, 0)
+    begin_ring(DOWN)
     pass_pairs(1)
-    begin_ring(DOWN)
     share_ring(3)
     take_unit(0, 1)
     forward_ring(UP)
@@ -385,13 +388,12 @@
             finish_ring(i, quarter)
 
     def heads(q, k, v):
+        def cut(value, unit, head):
+            return value[unit * 256 : unit * 256 + 256, head * HEAD : head * HEAD + HEAD]
+
+        found = attend([[cut(x, unit, head) for x in (q, k, v)] for unit in range(2) for head in range(3)])
         for unit in range(2):
-            rows = slice(unit * 256, unit * 256 + 256)
-            parts = []
-            for head in range(3):
-                columns = slice(head * HEAD, head * HEAD + HEAD)
-                parts.append(attend(q[rows, columns], k[rows, columns], v[rows, columns]))
-            mixed[rows, :] = jnp.concatenate(parts, axis=1)
+            mixed[unit * 256 : unit * 256 + 256, :] = jnp.concatenate(found[3 * unit : 3 * unit + 3], axis=1)
 
     def self_group(group, carry):
         @pl.when(group == 1)
@@ -427,16 +429,15 @@
         @pl.when(i == 0)
         def _():
             share_ring(DOWN)
+
+        @pl.when(i == 2)
+        def _():
             swap_ring(UP, "across")
 
-        @pl.when(i == 1)
-        def _():
+        @pl.when(i == 3)
+        def _():
+            swap_ring(DOWN, "right")
             swap_ring(DOWN, "left")
-            swap_ring(DOWN, "right")
-
-        @pl.when(i == 3)
-        def _():
-            swap_ring(DOWN, "across")
 
         for n in range(1, TP):
 
@@ -469,6 +470,7 @@
     def mlp_group(i, carry):
         @pl.when(i == 1)
         def _():
+            swap_ring(DOWN, "across")
             finish_ring(UP, "right")
             finish_ring(DOWN, "right")
 

time: 141 us -> 137 us (0.972)
  Pallas kernels: 139 us -> 135 us
    pallas_call x1, Pallas kernels: 139 us -> 135 us  [per_device(): pl.pallas_call(kernel, out_shape=jax.ShapeDtypeStruct((img_dev, ROWS, D),...]
where the time goes in v5:
time: 137 us
  Pallas kernels  135 us (99%)
  local copies, waits for them, and re-layouts  1.77 us (1%)
    pallas_call x1, Pallas kernels, per_device(): pl.pallas_call(kernel, out_shape=jax.ShapeDtypeStruct((img_dev, ROWS, D),...  135 us

profile of v5, /device:TPU:1, one launch (start us, length us, event | category | flops | bytes accessed | tf_op | source)
XLA Modules:
  0.0 137.1 jit_solution(638414321178180048)
XLA Ops:
  0.0 135.3 %shard_map.118 = bf16[4,64,768]{2,1,0:T(8,128)(2,1)} custom-call(s32[2,128]{1,0:T(2,128)} %bitcast.9, s32[128]{0:T(128)} %row_ref.1, bf16[4,64,1024]{2,1,0:T(8,128)(2,1)} %tokens_ref.1, bf16[1024,768]{1,0:T(8,128)(2,1)} %embed_ref.1, f32[2,4,768]{2,1,0:T(4,128)} %gain_ref.1, f32[2,4,768]{2,1,0:T(4,128)} %bias_ref.1, bf16[2,576,768]{2,1,0:T(8,128)(2,1)} %bitcast.7, ...), custom_call_target="tpu_custom_call" | custom-call | tf_op jit(solution)/shard_map/pallas_call | solution.py:585
  135.3 1.8 %copy.14 = bf16[4,64,768]{2,1,0:T(8,128)(2,1)} copy(bf16[4,64,768]{2,1,0:T(8,128)(2,1)} %shard_map.118) | data formatting | bytes 786432

commit v6 on v5

--- a/solution.py
+++ b/solution.py
@@ -88,7 +88,6 @@
     state,
     normed,
     partner,
-    mixed,
     unit_send,
     unit_recv_0,
     unit_recv_1,
@@ -371,53 +370,58 @@
     begin_pairs(1)
     for quarter in QUARTERS[1:]:
         offer_ring(2, quarter)
+    begin_ring(DOWN)
     for step in range(TP):
         pair_pass(step, 0).wait_recv()
     take_unit(1, 0)
-    begin_ring(DOWN)
     pass_pairs(1)
     share_ring(3)
     take_unit(0, 1)
     forward_ring(UP)
+
+    for i in range(2):
+        for quarter in QUARTERS:
+            finish_ring(i, quarter)
+
+    def heads(q, k, v):
+        def cut(value, unit, head):
+            return value[unit * 256 : unit * 256 + 256, head * HEAD : head * HEAD + HEAD]
+
+        found = attend([[cut(x, unit, head) for x in (q, k, v)] for unit in range(q.shape[0] // 256) for head in range(3)])
+        return [jnp.concatenate(found[n : n + 3], axis=1) for n in range(0, len(found), 3)]
+
+    def self_group(unit, group, carry):
+        if unit == 0:
+
+            @pl.when(group == 3)
+            def _():
+                swap_ring(2, "right")
+                swap_ring(2, "left")
+                swap_ring(2, "across")
+
+        else:
+
+            @pl.when(group == 1)
+            def _():
+                share_ring(UP)
+                forward_ring(DOWN)
+
+            @pl.when(group == 3)
+            def _():
+                swap_ring(UP, "left")
+                swap_ring(UP, "right")
+
+        rows = pl.ds(unit * 256, 256)
+        qkv = dot_t(normed[rows, :], w_self[group]).astype(jnp.bfloat16)
+        found = heads(qkv[:, 0:192], qkv[:, 192:384], qkv[:, 384:576])
+        state[rows, :] += dot(found[0], w_so[group])
+        return carry
+
+    lax.fori_loop(0, TP, functools.partial(self_group, 0), 0)
     for step in range(TP):
         pair_pass(step, 1).wait_recv()
     take_unit(1, 1)
-
-    for i in range(2):
-        for quarter in QUARTERS:
-            finish_ring(i, quarter)
-
-    def heads(q, k, v):
-        def cut(value, unit, head):
-            return value[unit * 256 : unit * 256 + 256, head * HEAD : head * HEAD + HEAD]
-
-        found = attend([[cut(x, unit, head) for x in (q, k, v)] for unit in range(2) for head in range(3)])
-        for unit in range(2):
-            mixed[unit * 256 : unit * 256 + 256, :] = jnp.concatenate(found[3 * unit : 3 * unit + 3], axis=1)
-
-    def self_group(group, carry):
-        @pl.when(group == 1)
-        def _():
-            swap_ring(2, "right")
-            swap_ring(2, "left")
-            swap_ring(2, "across")
-
-        @pl.when(group == 2)
-        def _():
-            share_ring(UP)
-            forward_ring(DOWN)
-
-        @pl.when(group == 3)
-        def _():
-            swap_ring(UP, "left")
-            swap_ring(UP, "right")
-
-        qkv = dot_t(normed[...], w_self[group]).astype(jnp.bfloat16)
-        heads(qkv[:, 0:192], qkv[:, 192:384], qkv[:, 384:576])
-        state[...] += dot(mixed[...], w_so[group])
-        return carry
-
-    lax.fori_loop(0, TP, self_group, 0)
+    lax.fori_loop(0, TP, functools.partial(self_group, 1), 0)
 
     for unit in range(2):
         rows = pl.ds(unit * 256, 256)
@@ -449,8 +453,8 @@
         group = lax.rem(t + i * (i + 1) // 2, TP)
         q = dot_t(normed[...], w_cross[group, 0:192]).astype(jnp.bfloat16)
         kv = dot_t(partner[...], w_cross[group, 192:576]).astype(jnp.bfloat16)
-        heads(q, kv[:, 0:192], kv[:, 192:384])
-        state[...] += dot(mixed[...], w_co[group])
+        found = heads(q, kv[:, 0:192], kv[:, 192:384])
+        state[...] += dot(jnp.concatenate(found, axis=0), w_co[group])
         return carry
 
     lax.fori_loop(0, TP, cross_group, 0)
@@ -598,7 +602,6 @@
             pltpu.VMEM((512, D), jnp.float32),
             pltpu.VMEM((512, D), bf16),
             pltpu.VMEM((512, D), bf16),
-            pltpu.VMEM((512, 192), bf16),
             pltpu.VMEM((2, TP, ROWS, D), bf16),
             pltpu.VMEM((4, 2, PART, D), bf16),
             pltpu.VMEM((4, 2, PART, D), bf16),

time: 137 us -> 136 us (level)
  no operation moved by 1% of the time
where the time goes in v6:
time: 136 us
  Pallas kernels  134 us (99%)
  local copies, waits for them, and re-layouts  1.77 us (1%)
    pallas_call x1, Pallas kernels, per_device(): pl.pallas_call(kernel, out_shape=jax.ShapeDtypeStruct((img_dev, ROWS, D),...  134 us

profile of v6, /device:TPU:1, one launch (start us, length us, event | category | flops | bytes accessed | tf_op | source)
XLA Modules:
  0.0 136.0 jit_solution(18418853546648576597)
XLA Ops:
  0.0 134.2 %shard_map.118 = bf16[4,64,768]{2,1,0:T(8,128)(2,1)} custom-call(s32[2,128]{1,0:T(2,128)} %bitcast.9, s32[128]{0:T(128)} %row_ref.1, bf16[4,64,1024]{2,1,0:T(8,128)(2,1)} %tokens_ref.1, bf16[1024,768]{1,0:T(8,128)(2,1)} %embed_ref.1, f32[2,4,768]{2,1,0:T(4,128)} %gain_ref.1, f32[2,4,768]{2,1,0:T(4,128)} %bias_ref.1, bf16[2,576,768]{2,1,0:T(8,128)(2,1)} %bitcast.7, ...), custom_call_target="tpu_custom_call" | custom-call | tf_op jit(solution)/shard_map/pallas_call | solution.py:589
  134.2 1.8 %copy.14 = bf16[4,64,768]{2,1,0:T(8,128)(2,1)} copy(bf16[4,64,768]{2,1,0:T(8,128)(2,1)} %shard_map.118) | data formatting | bytes 786432
